TPU v7x, 128 devices: a whole 4x4x4 slice. The times are simulated.
128 devices in a mesh: dp: 16 (over z_hi, y, core), ctx: 8 (over z_lo, x).
Axes of the slice: x: 4, y: 4, z: 4 (z_hi: 2, z_lo: 2; z = z_hi * 2 + z_lo), core: 2. Of those that a mesh axis runs over, the one named last changes fastest.
Arguments:
- inputs: bfloat16 [16, 2048, 960], P('dp', 'ctx'), may hold values from -6 to 6
- cotangent: bfloat16 [16, 2048, 960], P('dp', 'ctx'), may hold values from -6 to 6
- span_order: int32 [16], replicated, may hold values from 0 to 15, each once
- w_qkv: float32 [960, 1600], P('ctx'), may hold values from -0.1875 to 0.1875
- qkv_first: float32 [960, 1600], P('ctx'), may hold values from -128 to 128
- qkv_second: float32 [960, 1600], P('ctx'), may hold values from 983.04 to 9830.4
- w_proj: float32 [960, 960], P('ctx'), may hold values from -0.5 to 0.5
- proj_first: float32 [960, 960], P('ctx'), may hold values from -48 to 48
- proj_second: float32 [960, 960], P('ctx'), may hold values from 157.2864 to 1572.864
- w_expand: float32 [960, 5120], P('ctx'), may hold values from -0.1875 to 0.1875
- expand_first: float32 [960, 5120], P('ctx'), may hold values from -48 to 48
- expand_second: float32 [960, 5120], P('ctx'), may hold values from 157.2864 to 1572.864
- w_down: float32 [2560, 960], P('ctx'), may hold values from -0.125 to 0.125
- down_first: float32 [2560, 960], P('ctx'), may hold values from -64 to 64
- down_second: float32 [2560, 960], P('ctx'), may hold values from 353.8944 to 3538.944
- gains: float32 [2, 960], P(None, 'ctx'), may hold values from 0.5 to 1.5
- gains_first: float32 [2, 960], P(None, 'ctx'), may hold values from -128 to 128
- gains_second: float32 [2, 960], P(None, 'ctx'), may hold values from 983.04 to 9830.4
Outputs:
- output: bfloat16 [16, 2048, 960], P('dp', 'ctx')
- input_grad: bfloat16 [16, 2048, 960], P('dp', 'ctx')
- new_qkv: float32 [960, 1600], P('ctx')
- qkv_mean: float32 [960, 1600], P('ctx')
- qkv_square: float32 [960, 1600], P('ctx')
- new_proj: float32 [960, 960], P('ctx')
- proj_mean: float32 [960, 960], P('ctx')
- proj_square: float32 [960, 960], P('ctx')
- new_expand: float32 [960, 5120], P('ctx')
- expand_mean: float32 [960, 5120], P('ctx')
- expand_square: float32 [960, 5120], P('ctx')
- new_down: float32 [2560, 960], P('ctx')
- down_mean: float32 [2560, 960], P('ctx')
- down_square: float32 [2560, 960], P('ctx')
- new_gains: float32 [2, 960], P(None, 'ctx')
- gains_mean: float32 [2, 960], P(None, 'ctx')
- gains_square: float32 [2, 960], P(None, 'ctx')
Inputs may be any that keep to these rules, and one draw needn't show every extreme that they name: Layout block r of every sequence is sequence block span_order[r] of 128 tokens; each number appears once.
All inputs are finite; a program needn't handle non-finite values.
Results may differ from a plain program's by a relative error of at most 0.015.
Values may be sent and summed in bfloat16 or wider, within the bound.
No kernel may reach another device: no remote copies, remote signals or barrier semaphores. Data moves between devices by JAX's collectives and lax.ppermute only.
A program may use at most 320 MiB of HBM per device.

v0:
```python
import functools
import math

import jax
import jax.numpy as jnp
from jax import lax
from jax.experimental import pallas as pl
from jax.experimental.pallas import tpu as pltpu
from jax.sharding import PartitionSpec as P

D = 960
HEADS = 15
KV_HEADS = 5
GROUP = HEADS // KV_HEADS
HEAD_DIM = 64
FF = 2560
STEP = 10
HALF = FF // 2
QKVW = D + 2 * KV_HEADS * HEAD_DIM


eps = 1e-05
rope_base = 100000.0
beta_first = 0.9
beta_second = 0.95
adam_eps = 1e-08
masked_score = -1e30
TALL_WIDE = (slice(0, 384), slice(384, 768))
TALL_NARROW = (slice(768, 864), slice(864, 960))
LATE = 1280
SPLIT = 2
LOG2E = math.log2(math.e)
TALL = 56
PADDED = 896
PROJ = 120
NEAR = 896
BESIDE = 768
ATTEND_FLOPS = 20 * 10**9
BACK_FLOPS = 25 * 10**9
FEED_FLOPS = 20 * 10**9
low = jnp.bfloat16


AXES = ("zh", "y", "core", "zl", "x")
CHIPS = ("zh", "y")
CTX = ("zl", "x")
CHIP_CTX = ("zh", "zl", "x")


def swap_cores(value):
    return lax.ppermute(value, "core", [(0, 1), (1, 0)])


def to_peer(value, axis, k):
    count = lax.axis_size(axis)
    return lax.ppermute(value, axis, [(i, i ^ k) for i in range(count)])


def double(piece, axis, k, side):
    bit = lax.axis_index(axis) // k % 2 == 0
    came = to_peer(piece, axis, k)
    return jnp.concatenate(
        [jnp.where(bit, piece, came), jnp.where(bit, came, piece)], axis=side
    )


def add_peer(piece, axis, k):
    return (piece.astype(jnp.float32) + to_peer(piece, axis, k).astype(jnp.float32)).astype(low)


def exchange(stack, axes):
    return lax.all_to_all(stack, axes, 0, 0, tiled=True)


def spread(piece, axes, count):
    return exchange(jnp.broadcast_to(piece[None], (count,) + piece.shape), axes)


def total(stack):
    return jnp.sum(stack.astype(jnp.float32), axis=0).astype(low)


def ordered(core, mine, theirs):
    first = core == 0
    return jnp.where(first, mine, theirs), jnp.where(first, theirs, mine)


def rope_tables(positions):
    halfway = HEAD_DIM // 2
    freqs = rope_base ** (-(jnp.arange(halfway, dtype=jnp.float32) * 2.0) / HEAD_DIM)
    angles = freqs[:, None] * positions.astype(jnp.float32)[None, :]
    return (jnp.cos(angles), jnp.sin(angles))


def rms_scale(rows):
    return lax.rsqrt(jnp.mean(rows * rows, axis=-1, keepdims=True) + eps)


def contract(left, right, left_axis, right_axis):
    return lax.dot_general(
        left,
        right,
        (((left_axis,), (right_axis,)), ((), ())),
        preferred_element_type=jnp.float32,
    )


def in_three(row):
    rows = []
    for _ in range(3):
        part = row.astype(low).astype(jnp.float32)
        rows.append(part)
        row = row - part
    return jnp.concatenate(rows + [jnp.zeros((13, row.shape[1]), jnp.float32)], axis=0).astype(low)


def prepare(order_ref, own_ref, rank_ref, corner_ref, hide_ref):
    slots = order_ref.shape[0]
    span = corner_ref.shape[0] // 2
    ahead = lax.broadcasted_iota(jnp.int32, (span, span), 0) - lax.broadcasted_iota(
        jnp.int32, (span, span), 1
    )
    for s in range(2):
        for t in range(2):
            gap = (own_ref[s] - own_ref[t]) * span
            corner_ref[s * span : (s + 1) * span, t * span : (t + 1) * span] = jnp.where(
                ahead + gap <= 0, 0.0, masked_score
            )
    left = lax.broadcasted_iota(jnp.int32, (1, 2 * span), 1) < span
    rows = [jnp.zeros((2, 2 * span), jnp.float32)]
    for s in range(2, slots):
        at = order_ref[lax.rem(2 * rank_ref[0] + s, slots)]
        one = jnp.where(at > own_ref[0], masked_score, 0.0)
        two = jnp.where(at > own_ref[1], masked_score, 0.0)
        rows.append(jnp.where(left, one, two))
    hide_ref[...] = jnp.concatenate(rows, axis=0).astype(low)


def load_keys(rank_ref, kv_ref, per):
    chunks, _, wide, local = kv_ref.shape
    columns, keys, values = [], [], []
    for c in range(0, chunks, per):
        block = jnp.concatenate(
            [kv_ref[lax.rem(rank_ref[0] + i, chunks), 0] for i in range(c, c + per)], axis=1
        )
        rows = block.T
        lane = lax.broadcasted_iota(jnp.int32, (per * local, wide), 1)
        span = lax.broadcasted_iota(jnp.int32, (per * local, wide), 0) // (local // 2) + 2 * c
        ones = ((lane >= HEAD_DIM) & (lane < HEAD_DIM + 3)) | (lane == HEAD_DIM + 16 + span)
        keys.append(jnp.where(lane < HEAD_DIM, rows, jnp.where(ones, 1.0, 0.0).astype(low)))
        ones = jnp.where(lane < 3, 1.0, 0.0).astype(low)
        values.append(jnp.where(lane >= HEAD_DIM, rows, ones))
        columns.append(block)
    return columns, keys, values


def score(c, keys, query, corner):
    scores = contract(keys[c], query, 1, 0)
    if c == 0:
        local = corner.shape[0]
        scores = jnp.concatenate([scores[:local] + corner, scores[local:]], axis=0)
    return scores


def attend_kernel(
    order_ref, own_ref, rank_ref, q_ref, kv_ref, o_ref, lse_ref, corner_ref, hide_ref
):
    @pl.when(pl.program_id(0) == 0)
    def _():
        prepare(order_ref, own_ref, rank_ref, corner_ref, hide_ref)

    local = q_ref.shape[1]
    columns, keys, _ = load_keys(rank_ref, kv_ref, 2)
    corner = corner_ref[...]
    hide = hide_ref[...]
    blank = jnp.zeros((16, local), low)
    ones = jnp.ones((16, columns[0].shape[1]), low)
    sides = [jnp.concatenate([block[HEAD_DIM:], ones], axis=0) for block in columns]
    for h in range(GROUP):
        part = slice(h * HEAD_DIM, (h + 1) * HEAD_DIM)
        query = jnp.concatenate([q_ref[part, :], blank, hide, blank, blank], axis=0)
        scores = [score(c, keys, query, corner) for c in range(len(keys))]
        top = None
        for block in scores:
            block = jnp.max(block.reshape(-1, 8, local), axis=0)
            top = block if top is None else jnp.maximum(top, block)
        top = jnp.max(top, axis=0, keepdims=True)
        mixed = None
        for c, block in enumerate(scores):
            block = contract(sides[c], jnp.exp2(block - top).astype(low), 1, 0)
            mixed = block if mixed is None else mixed + block
        sums = mixed[HEAD_DIM : HEAD_DIM + 1]
        o_ref[part, :] = (mixed[:HEAD_DIM] / sums).astype(low)
        lse_ref[h] = top + jnp.log2(sums)


def attend_back_kernel(
    order_ref,
    own_ref,
    rank_ref,
    q_ref,
    kv_ref,
    do_ref,
    o_ref,
    lse_ref,
    dq_ref,
    dkv_ref,
    corner_ref,
    hide_ref,
):
    @pl.when(pl.program_id(0) == 0)
    def _():
        prepare(order_ref, own_ref, rank_ref, corner_ref, hide_ref)

    per = 4
    local = q_ref.shape[1]
    chunks = kv_ref.shape[0]
    columns, keys, values = load_keys(rank_ref, kv_ref, per)
    corner = corner_ref[...]
    hide = hide_ref[...]
    blank = jnp.zeros((16, local), low)
    wide_blank = jnp.zeros((HEAD_DIM, local), low)
    terms = [None] * len(keys)
    for h in range(GROUP):
        part = slice(h * HEAD_DIM, (h + 1) * HEAD_DIM)
        query = q_ref[part, :]
        back = do_ref[part, :]
        delta = jnp.sum(
            back.astype(jnp.float32) * o_ref[part, :].astype(jnp.float32), axis=0, keepdims=True
        )
        query_side = jnp.concatenate([query, in_three(-lse_ref[h]), hide, blank, blank], axis=0)
        back_side = jnp.concatenate([in_three(-delta), blank, blank, blank, back], axis=0)
        pair = jnp.concatenate(
            [
                jnp.concatenate([query, wide_blank], axis=0).T,
                jnp.concatenate([wide_blank, back], axis=0).T,
            ],
            axis=0,
        )
        grad_query = None
        for c in range(len(keys)):
            weights = jnp.exp2(score(c, keys, query_side, corner))
            grad = (weights * contract(values[c], back_side, 1, 0)).astype(low)
            term = contract(jnp.concatenate([grad, weights.astype(low)], axis=1), pair, 1, 0)
            terms[c] = term if terms[c] is None else terms[c] + term
            term = contract(columns[c][:HEAD_DIM], grad, 1, 0)
            grad_query = term if grad_query is None else grad_query + term
        dq_ref[part, :] = grad_query * HEAD_DIM ** (-0.5)
    lane = lax.broadcasted_iota(jnp.int32, (1, 2 * HEAD_DIM), 1)
    scale = jnp.where(lane < HEAD_DIM, 1.0 / LOG2E, 1.0)
    for i in range(chunks):
        term = terms[i // per][i % per * local : (i % per + 1) * local]
        dkv_ref[lax.rem(rank_ref[0] + i, chunks), 0] = (term * scale).astype(low)


def attention_specs(chunks, local, start=0):
    wide = GROUP * HEAD_DIM
    heads = pl.BlockSpec((wide, local), lambda g: (g + start, 0))
    keys = pl.BlockSpec((chunks, 1, 2 * HEAD_DIM, local), lambda g: (0, g + start, 0, 0))
    sums = pl.BlockSpec((GROUP, 1, local), lambda g: (g + start, 0, 0))
    return heads, keys, sums


def scalars():
    return pl.BlockSpec(memory_space=pltpu.SMEM)


def attention_scratch(local, slots):
    return [pltpu.VMEM((local, local), jnp.float32), pltpu.VMEM((slots, local), low)]


def attend(order, own, rank, query, keys):
    chunks, _, _, local = keys.shape
    heads, kv, sums = attention_specs(chunks, local)
    return pl.pallas_call(
        attend_kernel,
        grid=(KV_HEADS,),
        out_shape=(
            jax.ShapeDtypeStruct((D, local), low),
            jax.ShapeDtypeStruct((HEADS, 1, local), jnp.float32),
        ),
        in_specs=[scalars(), scalars(), scalars(), heads, kv],
        out_specs=(heads, sums),
        scratch_shapes=attention_scratch(local, order.shape[0]),
        compiler_params=pltpu.CompilerParams(vmem_limit_bytes=60 * 1024 * 1024),
        cost_estimate=pl.CostEstimate(
            flops=ATTEND_FLOPS, bytes_accessed=1000, transcendentals=0
        ),
        name="attend",
    )(order, own, rank, query, keys)


def attend_back(start, count, order, own, rank, query, keys, back, out, lse):
    chunks, _, _, local = keys.shape
    heads, kv, sums = attention_specs(chunks, local, start)
    part, _, _ = attention_specs(chunks, local)
    grads = pl.BlockSpec((chunks, 1, local, 2 * HEAD_DIM), lambda g: (0, g, 0, 0))
    return pl.pallas_call(
        attend_back_kernel,
        grid=(count,),
        out_shape=(
            jax.ShapeDtypeStruct((count * GROUP * HEAD_DIM, local), jnp.float32),
            jax.ShapeDtypeStruct((chunks, count, local, 2 * HEAD_DIM), low),
        ),
        in_specs=[scalars(), scalars(), scalars(), heads, kv, heads, heads, sums],
        out_specs=(part, grads),
        scratch_shapes=attention_scratch(local, order.shape[0]),
        compiler_params=pltpu.CompilerParams(vmem_limit_bytes=60 * 1024 * 1024),
        cost_estimate=pl.CostEstimate(
            flops=BACK_FLOPS * count // KV_HEADS, bytes_accessed=1000, transcendentals=0
        ),
        name=f"attend_back_{start}",
    )(order, own, rank, query, keys, back, out, lse)


def whole_call(kernel, name, flops, out_shape, *operands, near=False):
    single = not isinstance(out_shape, tuple)
    shapes = (out_shape,) if single else out_shape
    far = [] if near else [i for i, value in enumerate(operands) if value.ndim > 1]
    away = [] if near else list(range(len(shapes)))
    space = pl.BlockSpec(memory_space=pltpu.VMEM if near else pltpu.HBM)

    def staged(*refs):
        ins = list(refs[: len(operands)])
        outs = list(refs[len(operands) : len(operands) + len(shapes)])
        scratch = refs[len(operands) + len(shapes) :]
        copies = []
        for k, i in enumerate(far):
            copies.append(pltpu.make_async_copy(ins[i], scratch[k], scratch[-2].at[k]))
            ins[i] = scratch[k]
        for copy in copies:
            copy.start()
        for copy in copies:
            copy.wait()
        held = outs if near else list(scratch[len(far) : len(far) + len(away)])
        kernel(*ins, *held)
        copies = [
            pltpu.make_async_copy(held[k], outs[k], scratch[-1].at[k]) for k in away
        ]
        for copy in copies:
            copy.start()
        for copy in copies:
            copy.wait()

    scratch = [pltpu.VMEM(operands[i].shape, operands[i].dtype) for i in far]
    scratch += [pltpu.VMEM(shapes[k].shape, shapes[k].dtype) for k in away]
    if not near:
        scratch += [pltpu.SemaphoreType.DMA((len(far),)), pltpu.SemaphoreType.DMA((len(away),))]
    outs = pl.pallas_call(
        staged,
        out_shape=shapes,
        in_specs=[scalars() if value.ndim == 1 else space for value in operands],
        out_specs=(space,) * len(shapes),
        scratch_shapes=scratch,
        compiler_params=pltpu.CompilerParams(vmem_limit_bytes=(24 if near else 60) * 1024 * 1024),
        cost_estimate=pl.CostEstimate(flops=flops, bytes_accessed=1000, transcendentals=0),
        name=name,
    )(*operands)
    return outs[0] if single else outs


def stage_kernel(core_ref, qkv_ref, gains_ref, near_ref):
    first = core_ref[0] == 0
    shard = qkv_ref.shape[0]
    gains = jnp.concatenate(
        [gains_ref[...], jnp.zeros((6, gains_ref.shape[1]), jnp.float32)], axis=0
    )
    gains = jnp.concatenate([gains, jnp.zeros((8, 128 - shard), jnp.float32)], axis=1).T
    near = jnp.concatenate(
        [
            jnp.where(first, qkv_ref[:, : QKVW // 2], qkv_ref[:, QKVW // 2 :]),
            gains[:shard, :2],
            jnp.zeros((shard, PADDED - QKVW // 2 - 2), jnp.float32),
        ],
        axis=1,
    ).astype(low)
    for j in range(near_ref.shape[0]):
        near_ref[j] = near


def stage_feed_kernel(place_ref, expand_ref, down_ref, proj_ref, wide_ref, tall_ref):
    first = place_ref[0] == 0
    step = FF // 16
    parts = []
    for k in range(4):
        left = expand_ref[:, 2 * k * step : (2 * k + 1) * step]
        right = expand_ref[:, (2 * k + 1) * step : (2 * k + 2) * step]
        parts.append(jnp.where(first, left, right))
    proj = jnp.where(first, proj_ref[:, : D // 2], proj_ref[:, D // 2 :])
    quarter = proj[:, :PROJ]
    for k in range(1, 4):
        quarter = jnp.where(place_ref[2] == k, proj[:, k * PROJ : (k + 1) * PROJ], quarter)
    blank = jnp.zeros((proj.shape[0], BESIDE - FF // 4 - PROJ), jnp.float32)
    wide = jnp.concatenate(parts + [quarter, blank], axis=1).astype(low)
    tall = down_ref[...].astype(low)
    for j in range(wide_ref.shape[0]):
        wide_ref[j] = wide
        tall_ref[j] = tall


def stage_feed(place, expand, down, proj, groups):
    shard = expand.shape[0]
    half = down.shape[0] // 2
    outs = [(groups, shard, BESIDE), (groups, half, D)]
    return pl.pallas_call(
        stage_feed_kernel,
        grid_spec=pltpu.PrefetchScalarGridSpec(
            num_scalar_prefetch=1,
            grid=(1,),
            in_specs=[
                pl.BlockSpec((shard, HALF), lambda i, place: (0, place[1])),
                pl.BlockSpec((half, D), lambda i, place: (place[0], 0)),
                pl.BlockSpec(proj.shape, lambda i, place: (0, 0)),
            ],
            out_specs=[pl.BlockSpec(out, lambda i, place: (0, 0, 0)) for out in outs],
        ),
        out_shape=[jax.ShapeDtypeStruct(out, low) for out in outs],
        compiler_params=pltpu.CompilerParams(vmem_limit_bytes=60 * 1024 * 1024),
        cost_estimate=pl.CostEstimate(flops=1000, bytes_accessed=8 * 10**6, transcendentals=0),
        name="stage_feed",
    )(place, expand, down, proj)


def rotated(block, cosine, sine):
    first = block[: HEAD_DIM // 2]
    second = block[HEAD_DIM // 2 :]
    return [first * cosine - second * sine, second * cosine + first * sine]


def project_kernel(
    core_ref,
    rows_ref,
    mine_ref,
    theirs_ref,
    cosine_ref,
    sine_ref,
    normed_ref,
    query_ref,
    keys_ref,
    gains_ref,
):
    first_core = core_ref[0] == 0
    cosine = cosine_ref[...]
    sine = sine_ref[...]
    rows = rows_ref[...].astype(jnp.float32).T
    gains = mine_ref[:, PADDED - 128 : PADDED].astype(jnp.float32).T
    at = QKVW // 2 - (PADDED - 128)
    gains_ref[...] = gains[at : at + 2]
    normed = (rows * rms_scale(rows) * gains[at : at + 1]).astype(low)
    normed_ref[...] = normed
    near = contract(normed, mine_ref[...], 1, 0).T
    away = contract(normed, theirs_ref[...], 1, 0).T
    half = QKVW // 2
    one = jnp.where(first_core, near, away)[:half]
    two = jnp.where(first_core, away, near)[:half]
    mixed = jnp.concatenate([one, two], axis=0)
    scale = HEAD_DIM ** (-0.5) * LOG2E
    for h in range(HEADS):
        span = slice(h * HEAD_DIM, (h + 1) * HEAD_DIM)
        turned = jnp.concatenate(rotated(mixed[span], cosine, sine), axis=0)
        query_ref[span] = (turned * scale).astype(low)
    for g in range(KV_HEADS):
        at = D + g * HEAD_DIM
        to = at + KV_HEADS * HEAD_DIM
        pair = rotated(mixed[at : at + HEAD_DIM], cosine, sine) + [mixed[to : to + HEAD_DIM]]
        pair = jnp.concatenate(pair, axis=0).astype(low)
        for j in range(keys_ref.shape[0]):
            keys_ref[j, g] = pair


def join_proj(ref):
    return jnp.concatenate([ref[q, :, :PROJ] for q in range(4)], axis=1)


def rows_kernel(own_ref, other_ref, out_ref):
    out_ref[...] = jnp.concatenate([own_ref[...], other_ref[...]], axis=1).T


def branch_kernel(mixed_ref, beside_ref, out_ref, proj_ref, sem):
    copy = pltpu.make_async_copy(beside_ref.at[:, :, pl.ds(FF // 4, 128)], proj_ref, sem)
    copy.start()
    copy.wait()
    product = contract(mixed_ref[...], join_proj(proj_ref), 1, 0)
    blank = jnp.zeros((product.shape[0], 512 - product.shape[1]), jnp.float32)
    out_ref[...] = jnp.concatenate([product, blank], axis=1).astype(low)


def branch(mixed, beside):
    rows, width = mixed.shape
    whole = pl.BlockSpec(memory_space=pltpu.VMEM)
    return pl.pallas_call(
        branch_kernel,
        out_shape=(
            jax.ShapeDtypeStruct((rows, 512), low),
            jax.ShapeDtypeStruct((4, width, 128), low),
        ),
        in_specs=[whole, pl.BlockSpec(memory_space=pltpu.HBM)],
        out_specs=(whole, whole),
        scratch_shapes=[pltpu.SemaphoreType.DMA(())],
        compiler_params=pltpu.CompilerParams(vmem_limit_bytes=60 * 1024 * 1024),
        cost_estimate=pl.CostEstimate(flops=1000, bytes_accessed=1000, transcendentals=0),
        name="branch",
    )(mixed, beside)


def middle_kernel(
    core_ref,
    near_ref,
    away_ref,
    rows_ref,
    other_ref,
    gains_ref,
    mid_ref,
    normed_ref,
    normed_other,
):
    first_core = core_ref[0] == 0
    local = rows_ref.shape[1]
    for at, rows, out in ((0, rows_ref, normed_ref), (local, other_ref, normed_other)):
        near = near_ref[at : at + local, : D // 2].astype(jnp.float32)
        away = away_ref[local - at : 2 * local - at, : D // 2].astype(jnp.float32)
        near, away = jnp.where(first_core, near, away), jnp.where(first_core, away, near)
        middle = rows[...].astype(jnp.float32).T + jnp.concatenate([near, away], axis=1)
        if at == 0:
            mid_ref[...] = middle
        out[...] = (middle * rms_scale(middle) * gains_ref[1:2]).astype(low)


def turn_kernel(
    core_ref,
    own_ref,
    came_ref,
    mid_ref,
    back_ref,
    gains_ref,
    mine_ref,
    theirs_ref,
    out_ref,
    grad_ref,
    grad_out_ref,
    kept_ref,
    sent_ref,
    gain_grad_ref,
):
    first_core = core_ref[0] == 0
    normed = own_ref[...] + came_ref[...].astype(jnp.float32)
    middle = mid_ref[...]
    inverse = rms_scale(middle)
    scaled = normed * gains_ref[1:2]
    inner = jnp.mean(scaled * middle, axis=-1, keepdims=True)
    grad = back_ref[...].astype(jnp.float32) + inverse * (
        scaled - middle * inverse * inverse * inner
    )
    grad_ref[...] = grad
    gain_grad_ref[...] = jnp.sum(normed * middle * inverse, axis=0, keepdims=True)
    one = grad[:, : D // 2]
    two = grad[:, D // 2 :]
    near = jnp.where(first_core, one, two).astype(low)
    away = jnp.where(first_core, two, one).astype(low)
    grad_out = contract(near, join_proj(mine_ref), 1, 1) + contract(
        away, join_proj(theirs_ref), 1, 1
    )
    grad_out_ref[...] = grad_out.T.astype(low)
    product = contract(out_ref[...], grad.astype(low), 1, 0)
    groups, window, _ = kept_ref.shape
    shard = product.shape[0] // groups
    for j in range(groups):
        top = product[j * shard : j * shard + window]
        bottom = product[(j + 1) * shard - window : (j + 1) * shard]
        kept_ref[j] = jnp.where(first_core, top, bottom).astype(low)
        sent_ref[j] = jnp.where(first_core, bottom, top).astype(low)


def emit_kernel(mid_ref, own_ref, came_ref, out_ref):
    value = mid_ref[...] + own_ref[...] + came_ref[...].astype(jnp.float32)
    out_ref[...] = value.T.astype(low)


def feed_kernel(
    rows_one,
    rows_two,
    back_one,
    back_two,
    expand_ref,
    down_ref,
    fed_ref,
    fed_other_ref,
    normed_ref,
    normed_other_ref,
    tall_ref,
    expand_grad_ref,
    rows_ref,
    back_ref,
    columns_ref,
    fed_sum,
    normed_sum,
):
    local = rows_one.shape[0]
    h = pl.program_id(0)

    @pl.when(h == 0)
    def _():
        rows_ref[:local] = rows_one[...]
        rows_ref[local:] = rows_two[...]
        back_ref[:local] = back_one[...]
        back_ref[local:] = back_two[...]
        columns_ref[...] = rows_ref[...].T

    rows = rows_ref[...]
    back = back_ref[...]
    columns = columns_ref[...]
    down = down_ref[...]
    step = down_ref.shape[0]
    wide = jnp.concatenate([expand_ref[0], expand_ref[1]], axis=1)
    both = contract(rows, wide, 1, 0)
    gate = both[:, :step]
    upward = both[:, step:]
    sigmoid = jax.nn.sigmoid(gate)
    active = gate * sigmoid
    hidden = (active * upward).astype(low)
    grad_hidden = contract(back, down, 1, 1)
    grad_up = (grad_hidden * active).astype(low)
    grad_gate = (grad_hidden * upward * sigmoid * (1.0 + gate * (1.0 - sigmoid))).astype(low)
    fed = contract(hidden, down, 1, 0)
    grad_both = jnp.concatenate([grad_gate, grad_up], axis=1)
    normed = contract(grad_both, wide, 1, 1)
    product = contract(hidden.T, back, 1, 0)
    quarter = FF // 64
    for y in range(4):
        tall_ref[y] = jnp.concatenate(
            [product[(4 * j + y) * quarter : (4 * j + y + 1) * quarter] for j in range(4)], axis=0
        ).astype(low)
    both = contract(columns, grad_both, 1, 0).astype(low)
    expand_grad_ref[0] = both[:, :step]
    expand_grad_ref[1] = both[:, step:]

    @pl.when(h == 0)
    def _():
        fed_sum[...] = fed
        normed_sum[...] = normed

    @pl.when(h == 1)
    def _():
        fed_all = fed_sum[...] + fed
        normed_all = normed_sum[...] + normed
        fed_ref[...] = fed_all[:local]
        fed_other_ref[...] = fed_all[local:].astype(low)
        normed_ref[...] = normed_all[:local]
        normed_other_ref[...] = normed_all[local:].astype(low)


def feed(rows, back, expand, down):
    local, width = rows[0].shape
    step = FF // 4
    held = pl.BlockSpec((local, width), lambda h: (0, 0))
    pair = pl.BlockSpec((2, width, step), lambda h: (h, 0, 0))
    tall = pl.BlockSpec((step, width), lambda h: (h, 0))
    rows_out = pl.BlockSpec((4, FF // 16, width), lambda h: (0, h, 0))
    own = jax.ShapeDtypeStruct((local, width), jnp.float32)
    other = jax.ShapeDtypeStruct((local, width), low)
    return pl.pallas_call(
        feed_kernel,
        grid=(2,),
        out_shape=(
            own,
            other,
            own,
            other,
            jax.ShapeDtypeStruct((4, 8 * TALL, width), low),
            jax.ShapeDtypeStruct((4, width, step), low),
        ),
        in_specs=[held] * 4 + [pair, tall],
        out_specs=(held,) * 4 + (rows_out, pair),
        scratch_shapes=[
            pltpu.VMEM((2 * local, width), low),
            pltpu.VMEM((2 * local, width), low),
            pltpu.VMEM((width, 2 * local), low),
            pltpu.VMEM((2 * local, width), jnp.float32),
            pltpu.VMEM((2 * local, width), jnp.float32),
        ],
        compiler_params=pltpu.CompilerParams(vmem_limit_bytes=60 * 1024 * 1024),
        cost_estimate=pl.CostEstimate(flops=FEED_FLOPS, bytes_accessed=1000, transcendentals=0),
        name="feed",
    )(*rows, *back, expand, down)


def stack_kernel(tall_in, kept_ref, came_ref, tall_ref, held, sem):
    proj = (kept_ref[...].astype(jnp.float32) + came_ref[...].astype(jnp.float32)).astype(low)
    rows = proj.shape[1] // 4
    for y in range(4):
        held[y] = jnp.concatenate(
            [proj[j, y * rows : (y + 1) * rows] for j in range(proj.shape[0])], axis=0
        )
    span = pl.ds(tall_ref.shape[1] - held.shape[1], held.shape[1])
    copy = pltpu.make_async_copy(held, tall_ref.at[:, span], sem)
    copy.start()
    copy.wait()


def stack(tall, kept, came):
    groups, window, width = kept.shape
    away = pl.BlockSpec(memory_space=pltpu.HBM)
    whole = pl.BlockSpec(memory_space=pltpu.VMEM)
    return pl.pallas_call(
        stack_kernel,
        out_shape=jax.ShapeDtypeStruct(tall.shape, low),
        in_specs=[away, whole, whole],
        out_specs=away,
        scratch_shapes=[
            pltpu.VMEM((4, groups * window // 4, width), low),
            pltpu.SemaphoreType.DMA(()),
        ],
        input_output_aliases={0: 0},
        compiler_params=pltpu.CompilerParams(vmem_limit_bytes=60 * 1024 * 1024),
        cost_estimate=pl.CostEstimate(flops=1000, bytes_accessed=1000, transcendentals=0),
        name="stack",
    )(tall, kept, came)


def adam_step(master, first, second, grad, rate, decay):
    new_first = beta_first * first + (1.0 - beta_first) * grad
    new_second = beta_second * second + (1.0 - beta_second) * grad * grad
    fix_one = 1.0 - beta_first**STEP
    fix_two = 1.0 - beta_second**STEP
    update = new_first / fix_one / (jnp.sqrt(new_second / fix_two) + adam_eps) + decay * master
    return (master - rate * update, new_first, new_second)


def update_kernel(
    core_ref,
    wide_ref,
    wide_other,
    rest_ref,
    rest_other,
    gains_ref,
    gains_first,
    gains_second,
    *refs,
):
    states, outs, gain_outs = refs[:12], refs[12:24], refs[24:27]
    held = refs[27:31]
    near = refs[31:35]
    load_sem, store_sem, near_sem = refs[35:]
    grads = (wide_ref, wide_other, rest_ref, rest_other)
    fetches = [pltpu.make_async_copy(grads[k], near[k], near_sem.at[k]) for k in range(4)]
    wide_ref, wide_other, rest_ref, rest_other = near
    first_core = core_ref[0] == 0
    shard = gains_ref.shape[1]
    quarter = held[3].shape[1] // 8

    def both(mine, theirs):
        return (
            jnp.where(first_core, mine, theirs).astype(jnp.float32),
            jnp.where(first_core, theirs, mine).astype(jnp.float32),
        )

    def expand_grad(q):
        step = FF // 16
        one, two = both(rest_ref[q, :shard, : FF // 4], rest_other[q, :shard, : FF // 4])
        parts = []
        for k in range(4):
            span = slice(k * step, (k + 1) * step)
            parts += [one[:, span], two[:, span]]
        return jnp.concatenate(parts, axis=1)

    def tall_grads():
        parts = [both(tall_part(rest_ref, q), tall_part(rest_other, q)) for q in range(4)]
        one = [part[0] for part in parts]
        two = [part[1] for part in parts]
        down = jnp.concatenate([part[:quarter] for part in one + two], axis=0)
        proj = jnp.concatenate(
            [part[TALL - 16 :] for part in one]
            + [two[0][TALL - 8 :]]
            + [part[TALL - 16 :] for part in two[1:]],
            axis=0,
        )
        return down, proj

    def wide_grad():
        one, two = both(wide_ref[:shard], wide_other[:shard])
        return jnp.concatenate([one[:, : QKVW // 2], two[:, : QKVW // 2]], axis=1)

    full = slice(None)
    pieces = [(2, pl.ds(i * HALF, HALF), 2.0 * D ** (-0.5)) for i in range(4)]
    pieces += [
        (3, full, 2.0 * FF ** (-0.5)),
        (1, full, 2.0 * (D // 8) ** (-0.5)),
        (0, full, 2.0 * D ** (-0.5)),
    ]

    def copies(p, out):
        weight, columns, _ = pieces[p]
        for k in range(3):
            near = held[weight].at[k, :, columns]
            if out:
                yield pltpu.make_async_copy(
                    near, outs[3 * weight + k].at[:, columns], store_sem.at[p, k]
                )
            else:
                yield pltpu.make_async_copy(
                    states[3 * weight + k].at[:, columns], near, load_sem.at[p, k]
                )

    for copy in fetches:
        copy.start()
    for p in range(len(pieces)):
        for copy in copies(p, False):
            copy.start()
    for copy in fetches:
        copy.wait()
    down, proj = tall_grads()
    for p, (weight, columns, rate) in enumerate(pieces):
        for copy in copies(p, False):
            copy.wait()
        if p < 4:
            grad = expand_grad(p % 2 * 2 + p // 2)
        else:
            grad = (down, proj)[p - 4] if p < 6 else wide_grad()
        new = adam_step(*[held[weight][k, :, columns] for k in range(3)], grad, rate, 0.1)
        for k in range(3):
            held[weight][k, :, columns] = new[k]
        for copy in copies(p, True):
            copy.start()
    one, two = both(wide_ref[...], wide_other[...])
    grad = one[shard : shard + 2, :shard] + two[shard : shard + 2, :shard]
    new = adam_step(gains_ref[...], gains_first[...], gains_second[...], grad, 1.0, 0.0)
    for out, value in zip(gain_outs, new):
        out[...] = value
    for p in range(len(pieces)):
        for copy in copies(p, True):
            copy.wait()


def update(core, wide, wide_other, rest, rest_other, gains, states):
    whole = pl.BlockSpec(memory_space=pltpu.VMEM)
    away = pl.BlockSpec(memory_space=pltpu.HBM)
    shapes = [jax.ShapeDtypeStruct(value.shape, jnp.float32) for value in states + gains]
    return pl.pallas_call(
        update_kernel,
        out_shape=shapes,
        in_specs=[scalars()] + [away] * 4 + [whole] * 3 + [away] * 12,
        out_specs=[away] * 12 + [whole] * 3,
        scratch_shapes=[
            pltpu.VMEM((3,) + states[3 * weight].shape, jnp.float32) for weight in range(4)
        ]
        + [pltpu.VMEM(value.shape, low) for value in (wide, wide, rest, rest)]
        + [pltpu.SemaphoreType.DMA(shape) for shape in ((7, 3), (7, 3), (4,))],
        compiler_params=pltpu.CompilerParams(vmem_limit_bytes=32 * 1024 * 1024),
        cost_estimate=pl.CostEstimate(
            flops=1000, bytes_accessed=30 * 10**6, transcendentals=0
        ),
        name="update",
    )(core, wide, wide_other, rest, rest_other, *gains, *states)


def back_rotated(block, cosine, sine):
    first = block[: HEAD_DIM // 2]
    second = block[HEAD_DIM // 2 :]
    return [first * cosine + second * sine, second * cosine - first * sine]


def late_kernel(
    core_ref,
    first_terms,
    second_terms,
    first_dq,
    second_dq,
    cosine_ref,
    sine_ref,
    mine_ref,
    theirs_ref,
    rows_ref,
    grad_ref,
    gain_ref,
    gain_grad_ref,
    out_ref,
    near_ref,
    away_ref,
    gains_ref,
):
    cosine = cosine_ref[...]
    sine = sine_ref[...]
    first_core = core_ref[0] == 0
    parts = []
    for ref in (first_dq, second_dq):
        for h in range(ref.shape[0] // HEAD_DIM):
            parts += back_rotated(ref[h * HEAD_DIM : (h + 1) * HEAD_DIM], cosine, sine)
    values = []
    for ref in (first_terms, second_terms):
        for g in range(ref.shape[1]):
            block = ref[0, g].astype(jnp.float32)
            for j in range(1, ref.shape[0]):
                block = block + ref[j, g].astype(jnp.float32)
            block = block.T
            parts += back_rotated(block[:HEAD_DIM], cosine, sine)
            values.append(block[HEAD_DIM:])
    mixed = jnp.concatenate(parts + values, axis=0)
    half = QKVW // 2
    blank = jnp.zeros((PADDED - half, mixed.shape[1]), jnp.float32)
    one = mixed[:half]
    two = mixed[half:]
    near = jnp.concatenate([jnp.where(first_core, one, two), blank], axis=0).T.astype(low)
    away = jnp.concatenate([jnp.where(first_core, two, one), blank], axis=0).T.astype(low)
    grad_normed = contract(near, mine_ref[...], 1, 1) + contract(away, theirs_ref[...], 1, 1)
    rows = rows_ref[...].astype(jnp.float32).T
    inverse = rms_scale(rows)
    scaled = grad_normed * gain_ref[0:1]
    inner = jnp.mean(scaled * rows, axis=-1, keepdims=True)
    back = inverse * (scaled - rows * inverse * inverse * inner)
    out_ref[...] = (grad_ref[...] + back).T.astype(low)
    gain_one = jnp.sum(grad_normed * rows * inverse, axis=0, keepdims=True)
    gains = (gain_one, gain_grad_ref[...])
    near_ref[...] = near
    away_ref[...] = away
    gains_ref[...] = jnp.concatenate(gains, axis=0)


def weight_kernel(
    normed_ref, normed_other, near_ref, came_ref, gains_ref, tall_ref, out_ref
):
    columns = jnp.concatenate([normed_ref[...], normed_other[...]], axis=0).T
    product = contract(columns, jnp.concatenate([near_ref[...], came_ref[...]], axis=0), 1, 0)
    groups = out_ref.shape[0] // 2
    shard = product.shape[0] // groups
    lanes = product.shape[1]
    gains = gains_ref[...]
    quarter = FF // 64
    down = tall_ref[: groups * quarter].astype(jnp.float32)
    proj = tall_ref[groups * quarter :].astype(jnp.float32)
    for j in range(groups):
        span = slice(j * shard, (j + 1) * shard)
        tail = padded_rows(gains[:, span], 128 - shard)
        tail = jnp.concatenate(
            [tail, jnp.zeros((128 - shard, lanes - shard), jnp.float32)], axis=1
        )
        summed = jnp.concatenate([product[span], tail], axis=0)
        tall = jnp.concatenate(
            [down[j * quarter : (j + 1) * quarter], proj[j * 16 : (j + 1) * 16]], axis=0
        )
        halves = [
            jnp.concatenate([padded_rows(tall[:, span], 64) for span in spans], axis=0)
            for spans in (TALL_NARROW, TALL_WIDE)
        ]
        put_halves(out_ref, j, jnp.concatenate([summed[:, : QKVW // 2]] + halves, axis=1))


def padded_rows(block, rows):
    return jnp.concatenate(
        [block, jnp.zeros((rows - block.shape[0], block.shape[1]), jnp.float32)], axis=0
    )


def put_halves(out_ref, j, block):
    groups = out_ref.shape[0] // 2
    rows = out_ref.shape[1]
    for half in range(2):
        out_ref[half * groups + j] = block[half * rows : (half + 1) * rows].astype(low)


def pack_early_kernel(expand_ref, out_ref):
    for j in range(expand_ref.shape[0]):
        put_halves(out_ref, j, padded_rows(expand_ref[j].astype(jnp.float32), 128))


def sum_kernel(early_ref, late_ref, out_ref):
    sums = []
    for ref in (early_ref, late_ref):
        block = ref[0].astype(jnp.float32)
        for j in range(1, ref.shape[0]):
            block = block + ref[j].astype(jnp.float32)
        sums.append(block.astype(low))
    block = jnp.concatenate(sums, axis=1)
    for j in range(out_ref.shape[0]):
        out_ref[j] = block


def finish_kernel(all_ref, wide_ref, rest_ref):
    count = all_ref.shape[0] // 2
    rows = all_ref.shape[1]
    expand = slice(0, FF // 4)
    wide = slice(FF // 4, FF // 4 + PADDED)
    tall = slice(FF // 4 + LATE - 512, FF // 4 + LATE)
    for half in range(2):
        span = slice(half * rows, (half + 1) * rows)
        block = all_ref[half * count, :, wide].astype(jnp.float32)
        for y in range(1, count):
            block = block + all_ref[half * count + y, :, wide].astype(jnp.float32)
        wide_ref[span] = block.astype(low)
        for y in range(count):
            rest_ref[y, span] = jnp.concatenate(
                [all_ref[half * count + y, :, lanes] for lanes in (expand, tall)], axis=1
            )


def tall_part(rest, q):
    parts = []
    for lanes in (slice(FF // 4 + 128, FF // 4 + 512), slice(FF // 4 + 32, FF // 4 + 128)):
        parts += [rest[q, at : at + TALL, lanes] for at in (0, rest.shape[1] // 2)]
    return jnp.concatenate(parts, axis=1)


def on_device(
    inputs,
    cotangent,
    span_order,
    w_qkv,
    qkv_first,
    qkv_second,
    w_proj,
    proj_first,
    proj_second,
    w_expand,
    expand_first,
    expand_second,
    w_down,
    down_first,
    down_second,
    gains,
    gains_first,
    gains_second,
):
    core = lax.axis_index("core")
    rank = lax.axis_index(CTX)
    groups = 8
    batch, local, width = inputs.shape
    shard = w_qkv.shape[0]
    hidden_shard = w_down.shape[0] // 2

    y = lax.axis_index("y")
    place = jnp.stack([core, y % 2 * 2 + y // 2, y]).astype(jnp.int32)
    core_at = place[:1]
    rank_at = rank.reshape(1).astype(jnp.int32)
    near = whole_call(
        stage_kernel,
        "stage",
        1000,
        jax.ShapeDtypeStruct((groups, shard, NEAR), low),
        core_at,
        w_qkv,
        gains,
    )
    mine = exchange(near, CTX).reshape(width, NEAR)
    expand_low, down_low = stage_feed(place, w_expand, w_down, w_proj, groups)
    back_rows = cotangent.reshape(local, width)
    order_own = lax.dynamic_slice_in_dim(span_order, 2 * rank, 2)
    own_pos = (
        order_own[:, None] * (local // 2) + jnp.arange(local // 2, dtype=jnp.int32)
    ).reshape(local)
    cosine, sine = rope_tables(own_pos)
    mine, cosine, sine, expand_low, down_low, back_rows = lax.optimization_barrier(
        (mine, cosine, sine, expand_low, down_low, back_rows)
    )
    theirs = swap_cores(mine)
    expand_low = exchange(expand_low, CTX).reshape(width, BESIDE)

    tokens = inputs.reshape(local, width).T
    square = (local, width)
    normed_one, query, all_keys, full_gains = whole_call(
        project_kernel,
        "project",
        1000,
        (
            jax.ShapeDtypeStruct(square, low),
            jax.ShapeDtypeStruct((width, local), low),
            jax.ShapeDtypeStruct((groups, KV_HEADS, 2 * HEAD_DIM, local), low),
            jax.ShapeDtypeStruct((2, width), jnp.float32),
        ),
        core_at,
        tokens,
        mine,
        theirs,
        cosine,
        sine,
    )
    all_keys, expand_low = lax.optimization_barrier((all_keys, expand_low))
    expand_low = lax.all_gather(expand_low, "y", axis=0, tiled=False)
    all_keys = exchange(all_keys, CTX)
    all_keys, down_low = lax.optimization_barrier((all_keys, down_low))
    normed_other = swap_cores(normed_one)
    tokens_other = swap_cores(tokens)
    half_down = exchange(down_low, CTX).reshape(HALF, width)
    attended, lse = attend(span_order, order_own, rank_at, query, all_keys)
    mixed = whole_call(
        rows_kernel,
        "rows",
        1000,
        jax.ShapeDtypeStruct((2 * local, width), low),
        attended,
        swap_cores(attended),
        near=True,
    )
    mixed, expand_low = lax.optimization_barrier((mixed, expand_low))
    mixed, proj_mine = branch(mixed, expand_low)
    middle, normed_two, normed_two_other = whole_call(
        middle_kernel,
        "middle",
        1000,
        (
            jax.ShapeDtypeStruct(square, jnp.float32),
            jax.ShapeDtypeStruct(square, low),
            jax.ShapeDtypeStruct(square, low),
        ),
        core_at,
        mixed,
        swap_cores(mixed),
        tokens,
        tokens_other,
        full_gains,
    )
    proj_theirs = swap_cores(proj_mine)
    normed_two, half_down = lax.optimization_barrier((normed_two, half_down))

    fed, fed_other, grad_normed, grad_other, tall, grad_expand = feed(
        (normed_two, normed_two_other),
        (back_rows, swap_cores(back_rows)),
        expand_low,
        half_down,
    )
    grad_middle, grad_att, proj_kept, proj_sent, gain_grad_two = whole_call(
        turn_kernel,
        "turn",
        3 * 10**9,
        (
            jax.ShapeDtypeStruct(square, jnp.float32),
            jax.ShapeDtypeStruct((width, local), low),
            jax.ShapeDtypeStruct((groups, 64, width), low),
            jax.ShapeDtypeStruct((groups, 64, width), low),
            jax.ShapeDtypeStruct((1, width), jnp.float32),
        ),
        core_at,
        grad_normed,
        swap_cores(grad_other),
        middle,
        back_rows,
        full_gains,
        proj_mine,
        proj_theirs,
        attended,
    )
    output = whole_call(
        emit_kernel,
        "emit",
        1000,
        jax.ShapeDtypeStruct((width, local), low),
        middle,
        fed,
        swap_cores(fed_other),
    )

    expand_sum = lax.psum_scatter(grad_expand, "y", scatter_dimension=0, tiled=False)
    context = (span_order, order_own, rank_at, query, all_keys, grad_att, attended, lse)
    first_query, first_terms = attend_back(0, SPLIT, *context)
    first_terms, tall = lax.optimization_barrier((first_terms, tall))
    first_terms = exchange(first_terms, CTX)
    grad_query, key_terms = attend_back(SPLIT, KV_HEADS - SPLIT, *context)
    key_terms = exchange(key_terms, CTX)
    early = whole_call(
        pack_early_kernel,
        "pack_early",
        1000,
        jax.ShapeDtypeStruct((2 * groups, 64, FF // 4), low),
        expand_sum.reshape(groups, shard, FF // 4),
    )
    key_terms, first_terms, output, early = lax.optimization_barrier(
        (key_terms, first_terms, output, early)
    )
    early = exchange(early, CHIP_CTX)
    tall = stack(tall, proj_kept, swap_cores(proj_sent))
    tall = lax.psum_scatter(tall, "y", scatter_dimension=0, tiled=False)
    half = jax.ShapeDtypeStruct((local, PADDED), low)
    input_grad, near, away, late_gains = whole_call(
        late_kernel,
        "late",
        30 * 10**9,
        (
            jax.ShapeDtypeStruct((width, local), low),
            half,
            half,
            jax.ShapeDtypeStruct((2, width), jnp.float32),
        ),
        core_at,
        first_terms,
        key_terms,
        first_query,
        grad_query,
        cosine,
        sine,
        mine,
        theirs,
        tokens,
        grad_middle,
        full_gains,
        gain_grad_two,
    )
    late = whole_call(
        weight_kernel,
        "weight",
        1000,
        jax.ShapeDtypeStruct((2 * groups, 64, LATE), low),
        normed_one,
        normed_other,
        near,
        swap_cores(away),
        late_gains,
        tall.reshape(groups * TALL, width),
    )
    late, early = lax.optimization_barrier((late, early))
    late = exchange(late, CHIP_CTX)
    parts = whole_call(
        sum_kernel,
        "sum_parts",
        1000,
        jax.ShapeDtypeStruct((8, 64, FF // 4 + LATE), low),
        early,
        late,
        near=True,
    )
    wide, rest = whole_call(
        finish_kernel,
        "finish",
        1000,
        (
            jax.ShapeDtypeStruct((128, PADDED), low),
            jax.ShapeDtypeStruct((4, 128, FF // 4 + 512), low),
        ),
        exchange(parts, CHIPS),
        near=True,
    )
    wide_other = swap_cores(wide)
    rest_other = swap_cores(rest)
    news = update(
        core_at,
        wide,
        wide_other,
        rest,
        rest_other,
        [gains, gains_first, gains_second],
        [
            w_qkv,
            qkv_first,
            qkv_second,
            w_proj,
            proj_first,
            proj_second,
            w_expand,
            expand_first,
            expand_second,
            w_down,
            down_first,
            down_second,
        ],
    )
    return (
        output.T.reshape(batch, local, width),
        input_grad.T.reshape(batch, local, width),
        *news,
    )


def solution(mesh):
    parts = jax.sharding.Mesh(mesh.devices.reshape(2, 4, 2, 2, 4), AXES)
    dp, ctx = ("zh", "y", "core"), CTX
    rows = P(dp, ctx, None)
    owned = P(ctx, None)
    split = P(None, ctx)
    return jax.shard_map(
        on_device,
        mesh=parts,
        in_specs=(rows, rows, P()) + (owned,) * 12 + (split,) * 3,
        out_specs=(rows, rows) + (owned,) * 12 + (split,) * 3,
        check_vma=False,
    )
```

profile of v0, /device:TPU:1, one launch (start us, length us, event | category | flops | bytes accessed | tf_op | source)
XLA Modules:
  0.0 357.9 jit_solution(2371466987216341740)
XLA Ops:
  7.2 2.6 stage.1
  9.8 6.2 %all-to-all-start = ((bf16[8,120,896]{2,1,0:T(8,128)(2,1)}), bf16[8,120,896]{2,1,0:T(8,128)(2,1)S(1)}, u32[]{:S(2)}, u32[]{:S(2)}) async-start(bf16[8,120,896]{2,1,0:T(8,128)(2,1)} %stage.1), calls=%async_computation | async-start | bytes 3440640 | tf_op jit(solution)/shard_map/all_to_all | solution.py:72
  16.6 4.9 %stage_feed.1 = (bf16[8,120,768]{2,1,0:T(8,128)(2,1)}, bf16[8,160,960]{2,1,0:T(8,128)(2,1)}) custom-call(s32[3]{0:T(128)} %pad_add_fusion.place_ref, f32[120,5120]{1,0:T(8,128)} %refs_6_.1, f32[320,960]{1,0:T(8,128)} %refs_9_.1, f32[120,960]{1,0:T(8,128)} %refs_3_.1), custom_call_target="tpu_custom_call" | custom-call | flops 1000 | bytes 8000000 | tf_op jit(solution)/shard_map/stage_feed/pallas_call | solution.py:405
  24.0 15.0 %all-to-all-done = bf16[8,120,896]{2,1,0:T(8,128)(2,1)S(1)} async-done(((bf16[8,120,896]{2,1,0:T(8,128)(2,1)}), bf16[8,120,896]{2,1,0:T(8,128)(2,1)S(1)}, u32[]{:S(2)}, u32[]{:S(2)}) %all-to-all-start) | async-done | bytes 1720352 | tf_op jit(solution)/shard_map/all_to_all | solution.py:72
  39.8 4.3 %all-to-all-start.1 = ((bf16[8,120,768]{2,1,0:T(8,128)(2,1)}), bf16[8,120,768]{2,1,0:T(8,128)(2,1)}, u32[]{:S(2)}, u32[]{:S(2)}) async-start(bf16[8,120,768]{2,1,0:T(8,128)(2,1)} %get-tuple-element.95), calls=%async_computation.1 | async-start | bytes 2949120 | tf_op jit(solution)/shard_map/all_to_all | solution.py:72
  45.4 5.8 %project.1 = (bf16[256,960]{1,0:T(8,128)(2,1)}, bf16[960,256]{1,0:T(8,128)(2,1)}, bf16[8,5,128,256]{3,2,1,0:T(8,128)(2,1)}, f32[2,960]{1,0:T(2,128)}) custom-call(s32[1]{0:T(128)} %bitcast.1.refs_0_.core_ref, bf16[960,256]{1,0:T(8,128)(2,1)} %bitcast.27, bf16[960,896]{1,0:T(8,128)(2,1)} %bitcast.23, bf16[960,896]{1,0:T(8,128)(2,1)} %copy-done.19, ...), custom_call_target="tpu_custom_call" | custom-call | flops 1000 | bytes 1000 | tf_op jit(solution)/shard_map/project/pallas_call | solution.py:349
  51.2 13.5 %all-to-all-done.1 = bf16[8,120,768]{2,1,0:T(8,128)(2,1)} async-done(((bf16[8,120,768]{2,1,0:T(8,128)(2,1)}), bf16[8,120,768]{2,1,0:T(8,128)(2,1)}, u32[]{:S(2)}, u32[]{:S(2)}) %all-to-all-start.1) | async-done | bytes 1474592 | tf_op jit(solution)/shard_map/all_to_all | solution.py:72
  64.7 36.3 %all_to_all.45.kv_ref = bf16[8,5,128,256]{3,2,1,0:T(8,128)(2,1)} all-to-all(bf16[8,5,128,256]{3,2,1,0:T(8,128)(2,1)} %get-tuple-element.96), channel_id=1, replica_groups=mesh['zh'=2,'y'=4,'core'=2,'zl'=2,'x'=4] {'zl','x'}, dimensions={0} | all-to-all | bytes 5242880 | tf_op jit(solution)/shard_map/all_to_all | solution.py:72
  101.0 4.4 %all-to-all-start.3 = ((bf16[8,160,960]{2,1,0:T(8,128)(2,1)}), bf16[8,160,960]{2,1,0:T(8,128)(2,1)}, u32[]{:S(2)}, u32[]{:S(2)}) async-start(bf16[8,160,960]{2,1,0:T(8,128)(2,1)} %get-tuple-element.106), calls=%async_computation.3 | async-start | bytes 5242880 | tf_op jit(solution)/shard_map/all_to_all | solution.py:72
  105.5 16.5 %attend.1 = (bf16[960,256]{1,0:T(8,128)(2,1)}, f32[15,1,256]{2,1,0:T(1,128)}) custom-call(s32[16]{0:T(128)} %order_ref.5, s32[2]{0:T(128)} %get-tuple-element.160.own_ref, s32[1]{0:T(128)} %bitcast.rank_ref, bf16[960,256]{1,0:T(8,128)(2,1)} %get-tuple-element.93.q_ref, bf16[8,5,128,256]{3,2,1,0:T(8,128)(2,1)} %all_to_all.45.kv_ref), custom_call_target="tpu_custom_call" | custom-call | flops 20000000000 | bytes 1000 | tf_op jit(solution)/shard_map/attend/pallas_call | solution.py:275
  129.2 4.1 %branch.1 = (bf16[512,512]{1,0:T(8,128)(2,1)}, bf16[4,960,128]{2,1,0:T(8,128)(2,1)}) custom-call(bf16[512,960]{1,0:T(8,128)(2,1)} %copy-done.2, bf16[4,960,768]{2,1,0:T(8,128)(2,1)} %bitcast.25), custom_call_target="tpu_custom_call" | custom-call | flops 1000 | bytes 1000 | tf_op jit(solution)/shard_map/branch/pallas_call | solution.py:491
  137.3 3.4 middle.1
  141.5 20.0 %feed.1 = (f32[256,960]{1,0:T(8,128)}, bf16[256,960]{1,0:T(8,128)(2,1)}, f32[256,960]{1,0:T(8,128)}, bf16[256,960]{1,0:T(8,128)(2,1)}, bf16[4,448,960]{2,1,0:T(8,128)(2,1)}, /*index=5*/bf16[4,960,640]{2,1,0:T(8,128)(2,1)}) custom-call(bf16[256,960]{1,0:T(8,128)(2,1)} %get-tuple-element.107.rows_one, bf16[256,960]{1,0:T(8,128)(2,1)} %get-tuple-element.108.rows_two, ...), custom_call_target="tpu_custom_call" | custom-call | flops 20000000000 | bytes 1000 | tf_op jit(solution)/shard_map/feed/pallas_call | solution.py:661
  163.2 2.1 collective-permute-done.6.refs_7_
  166.8 6.1 %turn.1 = (f32[256,960]{1,0:T(8,128)}, bf16[960,256]{1,0:T(8,128)(2,1)}, bf16[8,64,960]{2,1,0:T(8,128)(2,1)}, bf16[8,64,960]{2,1,0:T(8,128)(2,1)}, f32[1,960]{1,0:T(1,128)}) custom-call(s32[1]{0:T(128)} %bitcast.1.refs_0_.core_ref, f32[256,960]{1,0:T(8,128)} %get-tuple-element.111.refs_1_, bf16[256,960]{1,0:T(8,128)(2,1)} %copy-done.35, ...), custom_call_target="tpu_custom_call" | custom-call | flops 3000000000 | bytes 1000 | tf_op jit(solution)/shard_map/turn/pallas_call | solution.py:349
  173.6 10.6 %attend_back_0.1 = (f32[384,256]{1,0:T(8,128)}, bf16[8,2,256,128]{3,2,1,0:T(8,128)(2,1)}) custom-call(s32[16]{0:T(128)} %order_ref.5, s32[2]{0:T(128)} %get-tuple-element.160.own_ref, s32[1]{0:T(128)} %bitcast.rank_ref, bf16[960,256]{1,0:T(8,128)(2,1)} %get-tuple-element.93.q_ref, bf16[8,5,128,256]{3,2,1,0:T(8,128)(2,1)} %all_to_all.45.kv_ref, ...), custom_call_target="tpu_custom_call" | custom-call | flops 10000000000 | bytes 1000 | tf_op jit(solution)/shard_map/attend_back_0/pallas_call | solution.py:298
  185.2 2.8 stack.17
  188.0 5.0 %all-to-all-start.5 = ((bf16[8,2,256,128]{3,2,1,0:T(8,128)(2,1)}), bf16[8,2,256,128]{3,2,1,0:T(8,128)(2,1)S(1)}, u32[]{:S(2)}, u32[]{:S(2)}) async-start(bf16[8,2,256,128]{3,2,1,0:T(8,128)(2,1)} %get-tuple-element.120), calls=%async_computation.5 | async-start | bytes 2097152 | tf_op jit(solution)/shard_map/all_to_all | solution.py:72
  193.0 15.0 %attend_back_2.1 = (f32[576,256]{1,0:T(8,128)}, bf16[8,3,256,128]{3,2,1,0:T(8,128)(2,1)}) custom-call(s32[16]{0:T(128)} %order_ref.5, s32[2]{0:T(128)} %get-tuple-element.160.own_ref, s32[1]{0:T(128)} %bitcast.rank_ref, bf16[960,256]{1,0:T(8,128)(2,1)} %get-tuple-element.93.q_ref, bf16[8,5,128,256]{3,2,1,0:T(8,128)(2,1)} %all_to_all.45.kv_ref, ...), custom_call_target="tpu_custom_call" | custom-call | flops 15000000512 | bytes 1000 | tf_op jit(solution)/shard_map/attend_back_2/pallas_call | solution.py:298
  208.9 4.4 %all-to-all-start.4 = ((bf16[8,3,256,128]{3,2,1,0:T(8,128)(2,1)}), bf16[8,3,256,128]{3,2,1,0:T(8,128)(2,1)S(1)}, u32[]{:S(2)}, u32[]{:S(2)}) async-start(bf16[8,3,256,128]{3,2,1,0:T(8,128)(2,1)} %get-tuple-element.117), calls=%async_computation.4 | async-start | bytes 3145728 | tf_op jit(solution)/shard_map/all_to_all | solution.py:72
  216.7 2.7 emit.1
  219.5 2.5 pack_early.1
  222.0 12.7 %all-to-all-done.4.refs_2_ = bf16[8,3,256,128]{3,2,1,0:T(8,128)(2,1)S(1)} async-done(((bf16[8,3,256,128]{3,2,1,0:T(8,128)(2,1)}), bf16[8,3,256,128]{3,2,1,0:T(8,128)(2,1)S(1)}, u32[]{:S(2)}, u32[]{:S(2)}) %all-to-all-start.4) | async-done | bytes 1572896 | tf_op jit(solution)/shard_map/all_to_all | solution.py:72
  234.7 5.0 %all-to-all-start.6 = ((bf16[16,64,640]{2,1,0:T(8,128)(2,1)}), bf16[16,64,640]{2,1,0:T(8,128)(2,1)S(1)}, u32[]{:S(2)}, u32[]{:S(2)}) async-start(bf16[16,64,640]{2,1,0:T(8,128)(2,1)} %pack_early.1), calls=%async_computation.8 | async-start | bytes 2621440 | tf_op jit(solution)/shard_map/all_to_all | solution.py:72
  239.7 7.0 %late.1 = (bf16[960,256]{1,0:T(8,128)(2,1)}, bf16[256,896]{1,0:T(8,128)(2,1)}, bf16[256,896]{1,0:T(8,128)(2,1)}, f32[2,960]{1,0:T(2,128)}) custom-call(s32[1]{0:T(128)} %bitcast.1.refs_0_.core_ref, bf16[8,2,256,128]{3,2,1,0:T(8,128)(2,1)} %copy-done.22, bf16[8,3,256,128]{3,2,1,0:T(8,128)(2,1)} %copy-done.20, f32[384,256]{1,0:T(8,128)} %get-tuple-element.127.refs_3_, ...), custom_call_target="tpu_custom_call" | custom-call | flops 30000001024 | bytes 1000 | tf_op jit(solution)/shard_map/late/pallas_call | solution.py:349
  247.5 12.3 %reduce-scatter.5.cloned.1.call-done = bf16[1,448,960]{2,1,0:T(8,128)(2,1)} async-done(((bf16[4,448,960]{2,1,0:T(8,128)(2,1)}), bf16[1,448,960]{2,1,0:T(8,128)(2,1)}) %reduce-scatter.5.cloned.1.call-update) | async-done | bytes 860176 | tf_op jit(solution)/shard_map/reduce_scatter | solution.py:1169
  260.6 4.6 %weight.1 = bf16[16,64,1280]{2,1,0:T(8,128)(2,1)} custom-call(bf16[256,960]{1,0:T(8,128)(2,1)} %get-tuple-element.132.refs_0_, bf16[256,960]{1,0:T(8,128)(2,1)} %collective-permute-done.8.refs_1_, bf16[256,896]{1,0:T(8,128)(2,1)} %get-tuple-element.133.refs_2_, bf16[256,896]{1,0:T(8,128)(2,1)} %copy-done.28, f32[2,960]{1,0:T(2,128)} %get-tuple-element.135.refs_4_, ...), custom_call_target="tpu_custom_call" | custom-call | flops 1000 | bytes 1000 | tf_op jit(solution)/shard_map/weight/pallas_call | solution.py:349
  265.2 39.9 %all_to_all.46.refs_1_ = bf16[16,64,1280]{2,1,0:T(8,128)(2,1)S(1)} all-to-all(bf16[16,64,1280]{2,1,0:T(8,128)(2,1)} %weight.1), channel_id=1, replica_groups=mesh['zh'=2,'y'=4,'core'=2,'zl'=2,'x'=4] {'zh','zl','x'}, dimensions={0} | all-to-all | bytes 5242880 | tf_op jit(solution)/shard_map/all_to_all | solution.py:72
  305.6 28.8 %all_to_all.47.refs_0_ = bf16[8,64,1920]{2,1,0:T(8,128)(2,1)S(1)} all-to-all(bf16[8,64,1920]{2,1,0:T(8,128)(2,1)S(1)} %sum_parts.1), channel_id=1, replica_groups=mesh['zh'=2,'y'=4,'core'=2,'zl'=2,'x'=4] {'zh','y'}, dimensions={0} | all-to-all | bytes 3932160 | tf_op jit(solution)/shard_map/all_to_all | solution.py:72
  334.5 2.6 collective-permute-start.12
  337.3 2.7 collective-permute-done.11.wide_other
  340.1 10.8 %update.1 = (f32[120,1600]{1,0:T(8,128)}, f32[120,1600]{1,0:T(8,128)}, f32[120,1600]{1,0:T(8,128)}, f32[120,960]{1,0:T(8,128)}, f32[120,960]{1,0:T(8,128)}, /*in...) custom-call(s32[1]{0:T(128)} %bitcast.1.refs_0_.core_ref, ...), custom_call_target="tpu_custom_call" | custom-call | flops 1000 | bytes 30000000 | tf_op jit(solution)/shard_map/update/pallas_call | solution.py:838
  (115 shorter events, 28.8 us)
Async XLA Ops:
  9.8 29.2 %all-to-all-start = ((bf16[8,120,896]{2,1,0:T(8,128)(2,1)}), bf16[8,120,896]{2,1,0:T(8,128)(2,1)S(1)}, u32[]{:S(2)}, u32[]{:S(2)}) async-start(bf16[8,120,896]{2,1,0:T(8,128)(2,1)} %stage.1), calls=%async_computation | async-start | bytes 3440640 | tf_op jit(solution)/shard_map/all_to_all | solution.py:72
  39.0 5.2 %collective-permute-start = (bf16[960,896]{1,0:T(8,128)(2,1)S(1)}, bf16[960,896]{1,0:T(8,128)(2,1)S(1)}, u32[]{:S(2)}, u32[]{:S(2)}) collective-permute-start(bf16[960,896]{1,0:T(8,128)(2,1)S(1)} %bitcast.22), channel_id=1, source_target_pairs={{0,8},{8,0},{1,9},{9,1},{2,10},{10,2},{3,11},{11,3},{4,12},{12,4},... | collective-permute-start | bytes 5160968 | tf_op jit(solution)/shard_map/ppermute | solution.py:51
  39.8 24.8 %all-to-all-start.1 = ((bf16[8,120,768]{2,1,0:T(8,128)(2,1)}), bf16[8,120,768]{2,1,0:T(8,128)(2,1)}, u32[]{:S(2)}, u32[]{:S(2)}) async-start(bf16[8,120,768]{2,1,0:T(8,128)(2,1)} %get-tuple-element.95), calls=%async_computation.1 | async-start | bytes 2949120 | tf_op jit(solution)/shard_map/all_to_all | solution.py:72
  44.1 85.0 %all-gather.3.cloned.1.call-start = ((), (), s32[]{:S(2)}) async-start(), calls=%async_computation.13 | async-start | bytes 7372800 | tf_op jit(solution)/shard_map/all_gather | solution.py:1076
  101.0 39.7 %all-to-all-start.3 = ((bf16[8,160,960]{2,1,0:T(8,128)(2,1)}), bf16[8,160,960]{2,1,0:T(8,128)(2,1)}, u32[]{:S(2)}, u32[]{:S(2)}) async-start(bf16[8,160,960]{2,1,0:T(8,128)(2,1)} %get-tuple-element.106), calls=%async_computation.3 | async-start | bytes 5242880 | tf_op jit(solution)/shard_map/all_to_all | solution.py:72
  105.4 114.1 %reduce-scatter.3.cloned.1.call-start = ((), (), s32[]{:S(2)}) async-start(), calls=%async_computation.11 | async-start | bytes 6144000 | tf_op jit(solution)/shard_map/reduce_scatter | solution.py:1150
  121.9 3.7 %collective-permute-start.1 = (bf16[960,256]{1,0:T(8,128)(2,1)}, bf16[960,256]{1,0:T(8,128)(2,1)S(1)}, u32[]{:S(2)}, u32[]{:S(2)}) collective-permute-start(bf16[960,256]{1,0:T(8,128)(2,1)} %get-tuple-element.99.refs_0_.refs_8_.o_ref), channel_id=1, source_target_pairs={{0,8},{8,0},{1,9},{9,1},{2,10},{10,2},{3,11},{11,3},{4,12},{12,4},... | collective-permute-start | bytes 1474568 | tf_op jit(solution)/shard_map/ppermute | solution.py:51
  133.3 3.0 collective-permute-start.2
  134.1 2.2 collective-permute-start.3
  134.2 6.5 %collective-permute-start.4 = (bf16[256,960]{1,0:T(8,128)(2,1)S(1)}, bf16[256,960]{1,0:T(8,128)(2,1)S(1)}, u32[]{:S(2)}, u32[]{:S(2)}) collective-permute-start(bf16[256,960]{1,0:T(8,128)(2,1)S(1)} %bitcast.35), channel_id=1, source_target_pairs={{0,8},{8,0},{1,9},{9,1},{2,10},{10,2},{3,11},{11,3},{4,12},{12,4},... | collective-permute-start | bytes 1474568 | tf_op jit(solution)/shard_map/ppermute | solution.py:51
  161.6 98.2 %reduce-scatter.5.cloned.1.call-start = ((), (), s32[]{:S(2)}) async-start(), calls=%async_computation.12 | async-start | bytes 4587520 | tf_op jit(solution)/shard_map/reduce_scatter | solution.py:1169
  162.7 2.6 collective-permute-start.6
  163.1 2.9 collective-permute-start.5
  172.9 11.3 %collective-permute-start.10 = (bf16[8,64,960]{2,1,0:T(8,128)(2,1)}, bf16[8,64,960]{2,1,0:T(8,128)(2,1)S(1)}, u32[]{:S(2)}, u32[]{:S(2)}) collective-permute-start(bf16[8,64,960]{2,1,0:T(8,128)(2,1)} %get-tuple-element.138), channel_id=1, source_target_pairs={{0,8},{8,0},{1,9},{9,1},{2,10},{10,2},{3,11},{11,3},{4,12},{12,4},... | collective-permute-start | bytes 2949128 | tf_op jit(solution)/shard_map/ppermute | solution.py:51
  188.0 20.9 %all-to-all-start.5 = ((bf16[8,2,256,128]{3,2,1,0:T(8,128)(2,1)}), bf16[8,2,256,128]{3,2,1,0:T(8,128)(2,1)S(1)}, u32[]{:S(2)}, u32[]{:S(2)}) async-start(bf16[8,2,256,128]{3,2,1,0:T(8,128)(2,1)} %get-tuple-element.120), calls=%async_computation.5 | async-start | bytes 2097152 | tf_op jit(solution)/shard_map/all_to_all | solution.py:72
  208.9 25.8 %all-to-all-start.4 = ((bf16[8,3,256,128]{3,2,1,0:T(8,128)(2,1)}), bf16[8,3,256,128]{3,2,1,0:T(8,128)(2,1)S(1)}, u32[]{:S(2)}, u32[]{:S(2)}) async-start(bf16[8,3,256,128]{3,2,1,0:T(8,128)(2,1)} %get-tuple-element.117), calls=%async_computation.4 | async-start | bytes 3145728 | tf_op jit(solution)/shard_map/all_to_all | solution.py:72
  213.3 2.7 collective-permute-start.7
  214.4 33.1 %collective-permute-start.8 = (bf16[256,960]{1,0:T(8,128)(2,1)}, bf16[256,960]{1,0:T(8,128)(2,1)}, u32[]{:S(2)}, u32[]{:S(2)}) collective-permute-start(bf16[256,960]{1,0:T(8,128)(2,1)} %get-tuple-element.132.refs_0_), channel_id=1, source_target_pairs={{0,8},{8,0},{1,9},{9,1},{2,10},{10,2},{3,11},{11,3},{4,12},{12,4},... | collective-permute-start | bytes 1474568 | tf_op jit(solution)/shard_map/ppermute | solution.py:51
  234.7 30.4 %all-to-all-start.6 = ((bf16[16,64,640]{2,1,0:T(8,128)(2,1)}), bf16[16,64,640]{2,1,0:T(8,128)(2,1)S(1)}, u32[]{:S(2)}, u32[]{:S(2)}) async-start(bf16[16,64,640]{2,1,0:T(8,128)(2,1)} %pack_early.1), calls=%async_computation.8 | async-start | bytes 2621440 | tf_op jit(solution)/shard_map/all_to_all | solution.py:72
  246.7 13.1 %collective-permute-start.9 = (bf16[256,896]{1,0:T(8,128)(2,1)}, bf16[256,896]{1,0:T(8,128)(2,1)S(1)}, u32[]{:S(2)}, u32[]{:S(2)}) collective-permute-start(bf16[256,896]{1,0:T(8,128)(2,1)} %get-tuple-element.134), channel_id=1, source_target_pairs={{0,8},{8,0},{1,9},{9,1},{2,10},{10,2},{3,11},{11,3},{4,12},{12,4},... | collective-permute-start | bytes 1376264 | tf_op jit(solution)/shard_map/ppermute | solution.py:51
  265.1 74.8 %copy-start.8 = (f32[320,960]{1,0:T(8,128)S(1)}, f32[320,960]{1,0:T(8,128)}, u32[]{:S(2)}) copy-start(f32[320,960]{1,0:T(8,128)} %refs_11_.1) | copy-start | bytes 3686404
  265.2 74.8 %copy-start.9 = (f32[120,1600]{1,0:T(8,128)S(1)}, f32[120,1600]{1,0:T(8,128)}, u32[]{:S(2)}) copy-start(f32[120,1600]{1,0:T(8,128)} %refs_1_.3) | copy-start | bytes 2304004
  265.2 74.8 %copy-start.10 = (f32[120,1600]{1,0:T(8,128)S(1)}, f32[120,1600]{1,0:T(8,128)}, u32[]{:S(2)}) copy-start(f32[120,1600]{1,0:T(8,128)} %refs_2_.3) | copy-start | bytes 2304004
  265.2 74.8 %copy-start.12 = (f32[120,960]{1,0:T(8,128)S(1)}, f32[120,960]{1,0:T(8,128)}, u32[]{:S(2)}) copy-start(f32[120,960]{1,0:T(8,128)} %refs_5_.1) | copy-start | bytes 1382404
  305.1 35.0 %copy-start = (f32[120,5120]{1,0:T(8,128)S(1)}, f32[120,5120]{1,0:T(8,128)}, u32[]{:S(2)}) copy-start(f32[120,5120]{1,0:T(8,128)} %refs_6_.1) | copy-start | bytes 7372804
  305.1 35.0 %copy-start.3 = (f32[120,1600]{1,0:T(8,128)S(1)}, f32[120,1600]{1,0:T(8,128)}, u32[]{:S(2)}) copy-start(f32[120,1600]{1,0:T(8,128)} %refs_0_.1) | copy-start | bytes 2304004
  305.1 35.0 %copy-start.5 = (f32[120,5120]{1,0:T(8,128)S(1)}, f32[120,5120]{1,0:T(8,128)}, u32[]{:S(2)}) copy-start(f32[120,5120]{1,0:T(8,128)} %refs_8_.1) | copy-start | bytes 7372804
  305.1 35.0 %copy-start.7 = (f32[320,960]{1,0:T(8,128)S(1)}, f32[320,960]{1,0:T(8,128)}, u32[]{:S(2)}) copy-start(f32[320,960]{1,0:T(8,128)} %refs_10_.1) | copy-start | bytes 3686404
  305.1 35.0 %copy-start.11 = (f32[120,960]{1,0:T(8,128)S(1)}, f32[120,960]{1,0:T(8,128)}, u32[]{:S(2)}) copy-start(f32[120,960]{1,0:T(8,128)} %refs_4_.1) | copy-start | bytes 1382404
  305.6 34.5 %copy-start.4 = (f32[120,5120]{1,0:T(8,128)S(1)}, f32[120,5120]{1,0:T(8,128)}, u32[]{:S(2)}) copy-start(f32[120,5120]{1,0:T(8,128)} %refs_7_.1) | copy-start | bytes 7372804
  334.5 5.4 %collective-permute-start.12 = (bf16[4,128,1152]{2,1,0:T(8,128)(2,1)S(1)}, bf16[4,128,1152]{2,1,0:T(8,128)(2,1)S(1)}, u32[]{:S(2)}, u32[]{:S(2)}) collective-permute-start(bf16[4,128,1152]{2,1,0:T(8,128)(2,1)S(1)} %get-tuple-element.143.rest_ref), channel_id=1, source_target_pairs={{0,8},{8,0},{1,9},{9,1},{2,10},{10,2},{3,11},{11,3},{4,12},{12,4},... | collective-permute-start | bytes 3538952 | tf_op jit(solution)/shard_map/ppermute | solution.py:51
  337.2 2.8 collective-permute-start.11
  (26 other events, 88.2 us)
Sparse Core Ops, SparseCore 0:
  64.8 64.3 all-gather.2
  161.7 53.2 reduce-scatter.2
  217.5 42.2 reduce-scatter.4
where the time goes:
time: 365 us; the launch traced here: 358 us
  Pallas kernels  120 us (33%)
  blocking collectives  105 us (29%)
  waiting for transfers between devices  66 us (18%)
  starting transfers between devices  39.6 us (11%)
  between operations  14.7 us (4%)
  local copies, waits for them, and re-layouts  10.5 us (3%)
    all_to_all x3, blocking collectives, exchange(): return lax.all_to_all(stack, axes, 0, 0, tiled=True)  105 us
    all_to_all x6, waiting for transfers between devices, exchange(): return lax.all_to_all(stack, axes, 0, 0, tiled=True)  42.2 us
    pallas_call x11, Pallas kernels, whole_call(): pl.pallas_call(staged, out_shape=shapes, in_specs=[scalars() if value.ndi...  35.5 us
    all_to_all x6, starting transfers between devices, exchange(): return lax.all_to_all(stack, axes, 0, 0, tiled=True)  29.3 us
    pallas_call x2, Pallas kernels, attend_back(): pl.pallas_call(attend_back_kernel, grid=(count,), out_shape=(jax.ShapeDty...  25.6 us
    pallas_call x1, Pallas kernels, feed(): pl.pallas_call(feed_kernel, grid=(2,), out_shape=(own, other, own, other,...  20 us
    pallas_call x1, Pallas kernels, attend(): pl.pallas_call(attend_kernel, grid=(KV_HEADS,), out_shape=(jax.ShapeDtype...  16.5 us
    reduce_scatter x1, waiting for transfers between devices, on_device(): tall = lax.psum_scatter(tall, 'y', scatter_dimension=0, tiled=False)  12.3 us
  transfers between devices with their start and end apart: 22, of which 12 were waited for; matrix products, arithmetic and copies ran while one was open for 1% of the time, Pallas kernels for 24%

commit v1 on v0

--- a/solution.py
+++ b/solution.py
@@ -497,7 +497,7 @@
         in_specs=[whole, pl.BlockSpec(memory_space=pltpu.HBM)],
         out_specs=(whole, whole),
         scratch_shapes=[pltpu.SemaphoreType.DMA(())],
-        compiler_params=pltpu.CompilerParams(vmem_limit_bytes=60 * 1024 * 1024),
+        compiler_params=pltpu.CompilerParams(vmem_limit_bytes=24 * 1024 * 1024),
         cost_estimate=pl.CostEstimate(flops=1000, bytes_accessed=1000, transcendentals=0),
         name="branch",
     )(mixed, beside)
@@ -756,7 +756,8 @@
 
     def expand_grad(q):
         step = FF // 16
-        one, two = both(rest_ref[q, :shard, : FF // 4], rest_other[q, :shard, : FF // 4])
+        one, two = both(rest_ref[q, :, : FF // 4], rest_other[q, :, : FF // 4])
+        one, two = one[:shard], two[:shard]
         parts = []
         for k in range(4):
             span = slice(k * step, (k + 1) * step)
@@ -764,9 +765,9 @@
         return jnp.concatenate(parts, axis=1)
 
     def tall_grads():
-        parts = [both(tall_part(rest_ref, q), tall_part(rest_other, q)) for q in range(4)]
-        one = [part[0] for part in parts]
-        two = [part[1] for part in parts]
+        parts = [both(rest_ref[q], rest_other[q]) for q in range(4)]
+        one = [tall_part(part[0]) for part in parts]
+        two = [tall_part(part[1]) for part in parts]
         down = jnp.concatenate([part[:quarter] for part in one + two], axis=0)
         proj = jnp.concatenate(
             [part[TALL - 16 :] for part in one]
@@ -777,8 +778,9 @@
         return down, proj
 
     def wide_grad():
-        one, two = both(wide_ref[:shard], wide_other[:shard])
-        return jnp.concatenate([one[:, : QKVW // 2], two[:, : QKVW // 2]], axis=1)
+        one, two = both(wide_ref[...], wide_other[...])
+        half = QKVW // 2
+        return jnp.concatenate([one[:shard, :half], two[:shard, :half]], axis=1)
 
     full = slice(None)
     pieces = [(2, pl.ds(i * HALF, HALF), 2.0 * D ** (-0.5)) for i in range(4)]
@@ -992,10 +994,10 @@
             )
 
 
-def tall_part(rest, q):
+def tall_part(rest):
     parts = []
     for lanes in (slice(FF // 4 + 128, FF // 4 + 512), slice(FF // 4 + 32, FF // 4 + 128)):
-        parts += [rest[q, at : at + TALL, lanes] for at in (0, rest.shape[1] // 2)]
+        parts += [rest[at : at + TALL, lanes] for at in (0, rest.shape[0] // 2)]
     return jnp.concatenate(parts, axis=1)
 
 

time: 365 us -> 365 us (level)
  transfers between devices with their start and end apart: 22 -> 22, of which waited for: 12 -> 12; matrix products, arithmetic and copies ran while one was open for 1% -> 1% of each run, Pallas kernels for 24% -> 23%
where the time goes in v1:
time: 365 us; the launch traced here: 358 us
  Pallas kernels  117 us (32%)
  blocking collectives  105 us (29%)
  waiting for transfers between devices  68.8 us (19%)
  starting transfers between devices  39.1 us (11%)
  between operations  14.7 us (4%)
  local copies, waits for them, and re-layouts  11.5 us (3%)
    all_to_all x3, blocking collectives, exchange(): return lax.all_to_all(stack, axes, 0, 0, tiled=True)  105 us
    all_to_all x6, waiting for transfers between devices, exchange(): return lax.all_to_all(stack, axes, 0, 0, tiled=True)  43.5 us
    pallas_call x11, Pallas kernels, whole_call(): pl.pallas_call(staged, out_shape=shapes, in_specs=[scalars() if value.ndi...  35.6 us
    all_to_all x6, starting transfers between devices, exchange(): return lax.all_to_all(stack, axes, 0, 0, tiled=True)  28.6 us
    pallas_call x2, Pallas kernels, attend_back(): pl.pallas_call(attend_back_kernel, grid=(count,), out_shape=(jax.ShapeDty...  25.6 us
    pallas_call x1, Pallas kernels, feed(): pl.pallas_call(feed_kernel, grid=(2,), out_shape=(own, other, own, other,...  20 us
    pallas_call x1, Pallas kernels, attend(): pl.pallas_call(attend_kernel, grid=(KV_HEADS,), out_shape=(jax.ShapeDtype...  16.5 us
    reduce_scatter x1, waiting for transfers between devices, on_device(): tall = lax.psum_scatter(tall, 'y', scatter_dimension=0, tiled=False)  12.9 us
  transfers between devices with their start and end apart: 22, of which 12 were waited for; matrix products, arithmetic and copies ran while one was open for 1% of the time, Pallas kernels for 23%

profile of v1, /device:TPU:1, one launch (start us, length us, event | category | flops | bytes accessed | tf_op | source)
XLA Modules:
  0.0 358.2 jit_solution(13408385421728550223)
XLA Ops:
  7.2 2.6 stage.1
  9.8 6.2 %all-to-all-start = ((bf16[8,120,896]{2,1,0:T(8,128)(2,1)}), bf16[8,120,896]{2,1,0:T(8,128)(2,1)S(1)}, u32[]{:S(2)}, u32[]{:S(2)}) async-start(bf16[8,120,896]{2,1,0:T(8,128)(2,1)} %stage.1), calls=%async_computation | async-start | bytes 3440640 | tf_op jit(solution)/shard_map/all_to_all | solution.py:72
  16.6 4.9 %stage_feed.1 = (bf16[8,120,768]{2,1,0:T(8,128)(2,1)}, bf16[8,160,960]{2,1,0:T(8,128)(2,1)}) custom-call(s32[3]{0:T(128)} %pad_add_fusion.place_ref, f32[120,5120]{1,0:T(8,128)} %refs_6_.1, f32[320,960]{1,0:T(8,128)} %refs_9_.1, f32[120,960]{1,0:T(8,128)} %refs_3_.1), custom_call_target="tpu_custom_call" | custom-call | flops 1000 | bytes 8000000 | tf_op jit(solution)/shard_map/stage_feed/pallas_call | solution.py:405
  24.0 15.0 %all-to-all-done = bf16[8,120,896]{2,1,0:T(8,128)(2,1)S(1)} async-done(((bf16[8,120,896]{2,1,0:T(8,128)(2,1)}), bf16[8,120,896]{2,1,0:T(8,128)(2,1)S(1)}, u32[]{:S(2)}, u32[]{:S(2)}) %all-to-all-start) | async-done | bytes 1720352 | tf_op jit(solution)/shard_map/all_to_all | solution.py:72
  39.8 3.6 all-to-all-start.1
  43.5 5.8 %project.1 = (bf16[256,960]{1,0:T(8,128)(2,1)}, bf16[960,256]{1,0:T(8,128)(2,1)}, bf16[8,5,128,256]{3,2,1,0:T(8,128)(2,1)}, f32[2,960]{1,0:T(2,128)}) custom-call(s32[1]{0:T(128)} %bitcast.1.refs_0_.core_ref, bf16[960,256]{1,0:T(8,128)(2,1)} %bitcast.28, bf16[960,896]{1,0:T(8,128)(2,1)} %bitcast.25, bf16[960,896]{1,0:T(8,128)(2,1)} %collective-permute-done.refs_3_.refs_8_, ...), custom_call_target="tpu_custom_call" | custom-call | flops 1000 | bytes 1000 | tf_op jit(solution)/shard_map/project/pallas_call | solution.py:349
  49.3 14.6 %all-to-all-done.1 = bf16[8,120,768]{2,1,0:T(8,128)(2,1)S(1)} async-done(((bf16[8,120,768]{2,1,0:T(8,128)(2,1)}), bf16[8,120,768]{2,1,0:T(8,128)(2,1)S(1)}, u32[]{:S(2)}, u32[]{:S(2)}) %all-to-all-start.1) | async-done | bytes 1474592 | tf_op jit(solution)/shard_map/all_to_all | solution.py:72
  65.0 36.3 %all_to_all.45.kv_ref = bf16[8,5,128,256]{3,2,1,0:T(8,128)(2,1)} all-to-all(bf16[8,5,128,256]{3,2,1,0:T(8,128)(2,1)} %get-tuple-element.96), channel_id=1, replica_groups=mesh['zh'=2,'y'=4,'core'=2,'zl'=2,'x'=4] {'zl','x'}, dimensions={0} | all-to-all | bytes 5242880 | tf_op jit(solution)/shard_map/all_to_all | solution.py:72
  101.3 4.4 %all-to-all-start.3 = ((bf16[8,160,960]{2,1,0:T(8,128)(2,1)}), bf16[8,160,960]{2,1,0:T(8,128)(2,1)}, u32[]{:S(2)}, u32[]{:S(2)}) async-start(bf16[8,160,960]{2,1,0:T(8,128)(2,1)} %get-tuple-element.106), calls=%async_computation.3 | async-start | bytes 5242880 | tf_op jit(solution)/shard_map/all_to_all | solution.py:72
  105.8 16.5 %attend.1 = (bf16[960,256]{1,0:T(8,128)(2,1)}, f32[15,1,256]{2,1,0:T(1,128)}) custom-call(s32[16]{0:T(128)} %order_ref.5, s32[2]{0:T(128)} %get-tuple-element.160.own_ref, s32[1]{0:T(128)} %bitcast.rank_ref, bf16[960,256]{1,0:T(8,128)(2,1)} %get-tuple-element.93.q_ref, bf16[8,5,128,256]{3,2,1,0:T(8,128)(2,1)} %all_to_all.45.kv_ref), custom_call_target="tpu_custom_call" | custom-call | flops 20000000000 | bytes 1000 | tf_op jit(solution)/shard_map/attend/pallas_call | solution.py:275
  129.5 2.7 copy-done.1
  134.6 2.3 collective-permute-done.3.refs_4_
  137.9 3.4 middle.1
  142.1 20.0 %feed.1 = (f32[256,960]{1,0:T(8,128)}, bf16[256,960]{1,0:T(8,128)(2,1)}, f32[256,960]{1,0:T(8,128)}, bf16[256,960]{1,0:T(8,128)(2,1)}, bf16[4,448,960]{2,1,0:T(8,128)(2,1)}, /*index=5*/bf16[4,960,640]{2,1,0:T(8,128)(2,1)}) custom-call(bf16[256,960]{1,0:T(8,128)(2,1)} %get-tuple-element.107.rows_one, bf16[256,960]{1,0:T(8,128)(2,1)} %get-tuple-element.108.rows_two, ...), custom_call_target="tpu_custom_call" | custom-call | flops 20000000000 | bytes 1000 | tf_op jit(solution)/shard_map/feed/pallas_call | solution.py:661
  166.4 6.2 %turn.1 = (f32[256,960]{1,0:T(8,128)}, bf16[960,256]{1,0:T(8,128)(2,1)}, bf16[8,64,960]{2,1,0:T(8,128)(2,1)}, bf16[8,64,960]{2,1,0:T(8,128)(2,1)}, f32[1,960]{1,0:T(1,128)}) custom-call(s32[1]{0:T(128)} %bitcast.1.refs_0_.core_ref, f32[256,960]{1,0:T(8,128)} %get-tuple-element.111.refs_1_, bf16[256,960]{1,0:T(8,128)(2,1)} %copy-done.35, ...), custom_call_target="tpu_custom_call" | custom-call | flops 3000000000 | bytes 1000 | tf_op jit(solution)/shard_map/turn/pallas_call | solution.py:349
  173.3 10.6 %attend_back_0.1 = (f32[384,256]{1,0:T(8,128)}, bf16[8,2,256,128]{3,2,1,0:T(8,128)(2,1)}) custom-call(s32[16]{0:T(128)} %order_ref.5, s32[2]{0:T(128)} %get-tuple-element.160.own_ref, s32[1]{0:T(128)} %bitcast.rank_ref, bf16[960,256]{1,0:T(8,128)(2,1)} %get-tuple-element.93.q_ref, bf16[8,5,128,256]{3,2,1,0:T(8,128)(2,1)} %all_to_all.45.kv_ref, ...), custom_call_target="tpu_custom_call" | custom-call | flops 10000000000 | bytes 1000 | tf_op jit(solution)/shard_map/attend_back_0/pallas_call | solution.py:298
  184.9 2.9 stack.17
  187.8 5.0 %all-to-all-start.5 = ((bf16[8,2,256,128]{3,2,1,0:T(8,128)(2,1)}), bf16[8,2,256,128]{3,2,1,0:T(8,128)(2,1)S(1)}, u32[]{:S(2)}, u32[]{:S(2)}) async-start(bf16[8,2,256,128]{3,2,1,0:T(8,128)(2,1)} %get-tuple-element.120), calls=%async_computation.5 | async-start | bytes 2097152 | tf_op jit(solution)/shard_map/all_to_all | solution.py:72
  192.8 15.0 %attend_back_2.1 = (f32[576,256]{1,0:T(8,128)}, bf16[8,3,256,128]{3,2,1,0:T(8,128)(2,1)}) custom-call(s32[16]{0:T(128)} %order_ref.5, s32[2]{0:T(128)} %get-tuple-element.160.own_ref, s32[1]{0:T(128)} %bitcast.rank_ref, bf16[960,256]{1,0:T(8,128)(2,1)} %get-tuple-element.93.q_ref, bf16[8,5,128,256]{3,2,1,0:T(8,128)(2,1)} %all_to_all.45.kv_ref, ...), custom_call_target="tpu_custom_call" | custom-call | flops 15000000512 | bytes 1000 | tf_op jit(solution)/shard_map/attend_back_2/pallas_call | solution.py:298
  208.7 4.4 %all-to-all-start.4 = ((bf16[8,3,256,128]{3,2,1,0:T(8,128)(2,1)}), bf16[8,3,256,128]{3,2,1,0:T(8,128)(2,1)S(1)}, u32[]{:S(2)}, u32[]{:S(2)}) async-start(bf16[8,3,256,128]{3,2,1,0:T(8,128)(2,1)} %get-tuple-element.117), calls=%async_computation.4 | async-start | bytes 3145728 | tf_op jit(solution)/shard_map/all_to_all | solution.py:72
  216.4 2.7 emit.1
  219.1 2.5 pack_early.1
  221.6 12.9 %all-to-all-done.4.refs_2_ = bf16[8,3,256,128]{3,2,1,0:T(8,128)(2,1)S(1)} async-done(((bf16[8,3,256,128]{3,2,1,0:T(8,128)(2,1)}), bf16[8,3,256,128]{3,2,1,0:T(8,128)(2,1)S(1)}, u32[]{:S(2)}, u32[]{:S(2)}) %all-to-all-start.4) | async-done | bytes 1572896 | tf_op jit(solution)/shard_map/all_to_all | solution.py:72
  234.5 5.0 %all-to-all-start.6 = ((bf16[16,64,640]{2,1,0:T(8,128)(2,1)}), bf16[16,64,640]{2,1,0:T(8,128)(2,1)S(1)}, u32[]{:S(2)}, u32[]{:S(2)}) async-start(bf16[16,64,640]{2,1,0:T(8,128)(2,1)} %pack_early.1), calls=%async_computation.8 | async-start | bytes 2621440 | tf_op jit(solution)/shard_map/all_to_all | solution.py:72
  239.5 7.0 %late.1 = (bf16[960,256]{1,0:T(8,128)(2,1)}, bf16[256,896]{1,0:T(8,128)(2,1)}, bf16[256,896]{1,0:T(8,128)(2,1)}, f32[2,960]{1,0:T(2,128)}) custom-call(s32[1]{0:T(128)} %bitcast.1.refs_0_.core_ref, bf16[8,2,256,128]{3,2,1,0:T(8,128)(2,1)} %copy-done.24, bf16[8,3,256,128]{3,2,1,0:T(8,128)(2,1)} %copy-done.22, f32[384,256]{1,0:T(8,128)} %get-tuple-element.127.refs_3_, ...), custom_call_target="tpu_custom_call" | custom-call | flops 30000001024 | bytes 1000 | tf_op jit(solution)/shard_map/late/pallas_call | solution.py:349
  247.2 12.9 %reduce-scatter.5.cloned.1.call-done = bf16[1,448,960]{2,1,0:T(8,128)(2,1)} async-done(((bf16[4,448,960]{2,1,0:T(8,128)(2,1)}), bf16[1,448,960]{2,1,0:T(8,128)(2,1)}) %reduce-scatter.5.cloned.1.call-update) | async-done | bytes 860176 | tf_op jit(solution)/shard_map/reduce_scatter | solution.py:1171
  260.9 4.5 %weight.1 = bf16[16,64,1280]{2,1,0:T(8,128)(2,1)} custom-call(bf16[256,960]{1,0:T(8,128)(2,1)} %get-tuple-element.132.refs_0_, bf16[256,960]{1,0:T(8,128)(2,1)} %collective-permute-done.8.refs_1_, bf16[256,896]{1,0:T(8,128)(2,1)} %get-tuple-element.133.refs_2_, bf16[256,896]{1,0:T(8,128)(2,1)} %copy-done.29, f32[2,960]{1,0:T(2,128)} %get-tuple-element.135.refs_4_, ...), custom_call_target="tpu_custom_call" | custom-call | flops 1000 | bytes 1000 | tf_op jit(solution)/shard_map/weight/pallas_call | solution.py:349
  265.5 39.9 %all_to_all.46.refs_1_ = bf16[16,64,1280]{2,1,0:T(8,128)(2,1)S(1)} all-to-all(bf16[16,64,1280]{2,1,0:T(8,128)(2,1)} %weight.1), channel_id=1, replica_groups=mesh['zh'=2,'y'=4,'core'=2,'zl'=2,'x'=4] {'zh','zl','x'}, dimensions={0} | all-to-all | bytes 5242880 | tf_op jit(solution)/shard_map/all_to_all | solution.py:72
  305.9 28.8 %all_to_all.47.refs_0_ = bf16[8,64,1920]{2,1,0:T(8,128)(2,1)S(1)} all-to-all(bf16[8,64,1920]{2,1,0:T(8,128)(2,1)S(1)} %sum_parts.1), channel_id=1, replica_groups=mesh['zh'=2,'y'=4,'core'=2,'zl'=2,'x'=4] {'zh','y'}, dimensions={0} | all-to-all | bytes 3932160 | tf_op jit(solution)/shard_map/all_to_all | solution.py:72
  334.9 2.6 collective-permute-start.12
  337.6 2.7 collective-permute-done.11.wide_other
  340.5 10.8 %update.1 = (f32[120,1600]{1,0:T(8,128)}, f32[120,1600]{1,0:T(8,128)}, f32[120,1600]{1,0:T(8,128)}, f32[120,960]{1,0:T(8,128)}, f32[120,960]{1,0:T(8,128)}, /*in...) custom-call(s32[1]{0:T(128)} %bitcast.1.refs_0_.core_ref, ...), custom_call_target="tpu_custom_call" | custom-call | flops 1000 | bytes 30000000 | tf_op jit(solution)/shard_map/update/pallas_call | solution.py:840
  (115 shorter events, 29.1 us)
Async XLA Ops:
  9.8 29.2 %all-to-all-start = ((bf16[8,120,896]{2,1,0:T(8,128)(2,1)}), bf16[8,120,896]{2,1,0:T(8,128)(2,1)S(1)}, u32[]{:S(2)}, u32[]{:S(2)}) async-start(bf16[8,120,896]{2,1,0:T(8,128)(2,1)} %stage.1), calls=%async_computation | async-start | bytes 3440640 | tf_op jit(solution)/shard_map/all_to_all | solution.py:72
  39.0 4.5 %collective-permute-start = (bf16[960,896]{1,0:T(8,128)(2,1)S(1)}, bf16[960,896]{1,0:T(8,128)(2,1)}, u32[]{:S(2)}, u32[]{:S(2)}) collective-permute-start(bf16[960,896]{1,0:T(8,128)(2,1)S(1)} %bitcast.24), channel_id=1, source_target_pairs={{0,8},{8,0},{1,9},{9,1},{2,10},{10,2},{3,11},{11,3},{4,12},{12,4},... | collective-permute-start | bytes 5160968 | tf_op jit(solution)/shard_map/ppermute | solution.py:51
  39.8 24.0 %all-to-all-start.1 = ((bf16[8,120,768]{2,1,0:T(8,128)(2,1)}), bf16[8,120,768]{2,1,0:T(8,128)(2,1)S(1)}, u32[]{:S(2)}, u32[]{:S(2)}) async-start(bf16[8,120,768]{2,1,0:T(8,128)(2,1)} %get-tuple-element.95), calls=%async_computation.1 | async-start | bytes 2949120 | tf_op jit(solution)/shard_map/all_to_all | solution.py:72
  43.4 86.1 %all-gather.3.cloned.1.call-start = ((), (), s32[]{:S(2)}) async-start(), calls=%async_computation.13 | async-start | bytes 7372800 | tf_op jit(solution)/shard_map/all_gather | solution.py:1078
  101.3 39.9 %all-to-all-start.3 = ((bf16[8,160,960]{2,1,0:T(8,128)(2,1)}), bf16[8,160,960]{2,1,0:T(8,128)(2,1)}, u32[]{:S(2)}, u32[]{:S(2)}) async-start(bf16[8,160,960]{2,1,0:T(8,128)(2,1)} %get-tuple-element.106), calls=%async_computation.3 | async-start | bytes 5242880 | tf_op jit(solution)/shard_map/all_to_all | solution.py:72
  105.7 113.4 %reduce-scatter.3.cloned.1.call-start = ((), (), s32[]{:S(2)}) async-start(), calls=%async_computation.11 | async-start | bytes 6144000 | tf_op jit(solution)/shard_map/reduce_scatter | solution.py:1152
  122.2 3.7 %collective-permute-start.1 = (bf16[960,256]{1,0:T(8,128)(2,1)}, bf16[960,256]{1,0:T(8,128)(2,1)S(1)}, u32[]{:S(2)}, u32[]{:S(2)}) collective-permute-start(bf16[960,256]{1,0:T(8,128)(2,1)} %get-tuple-element.99.refs_0_.refs_8_.o_ref), channel_id=1, source_target_pairs={{0,8},{8,0},{1,9},{9,1},{2,10},{10,2},{3,11},{11,3},{4,12},{12,4},... | collective-permute-start | bytes 1474568 | tf_op jit(solution)/shard_map/ppermute | solution.py:51
  133.2 3.7 %collective-permute-start.2 = (bf16[512,512]{1,0:T(8,128)(2,1)S(1)}, bf16[512,512]{1,0:T(8,128)(2,1)S(1)}, u32[]{:S(2)}, u32[]{:S(2)}) collective-permute-start(bf16[512,512]{1,0:T(8,128)(2,1)S(1)} %get-tuple-element.103.refs_1_), channel_id=1, source_target_pairs={{0,8},{8,0},{1,9},{9,1},{2,10},{10,2},{3,11},{11,3},{4,12},{12,4},... | collective-permute-start | bytes 1572872 | tf_op jit(solution)/shard_map/ppermute | solution.py:51
  134.0 2.9 collective-permute-start.3
  134.1 7.2 %collective-permute-start.4 = (bf16[256,960]{1,0:T(8,128)(2,1)}, bf16[256,960]{1,0:T(8,128)(2,1)S(1)}, u32[]{:S(2)}, u32[]{:S(2)}) collective-permute-start(bf16[256,960]{1,0:T(8,128)(2,1)} %bitcast.8.back_one.refs_4_), channel_id=1, source_target_pairs={{0,8},{8,0},{1,9},{9,1},{2,10},{10,2},{3,11},{11,3},{4,12},{12,4},... | collective-permute-start | bytes 1474568 | tf_op jit(solution)/shard_map/ppermute | solution.py:51
  162.1 98.0 %reduce-scatter.5.cloned.1.call-start = ((), (), s32[]{:S(2)}) async-start(), calls=%async_computation.12 | async-start | bytes 4587520 | tf_op jit(solution)/shard_map/reduce_scatter | solution.py:1171
  162.2 2.6 collective-permute-start.6
  163.1 2.4 collective-permute-start.5
  172.6 11.3 %collective-permute-start.10 = (bf16[8,64,960]{2,1,0:T(8,128)(2,1)}, bf16[8,64,960]{2,1,0:T(8,128)(2,1)S(1)}, u32[]{:S(2)}, u32[]{:S(2)}) collective-permute-start(bf16[8,64,960]{2,1,0:T(8,128)(2,1)} %get-tuple-element.138), channel_id=1, source_target_pairs={{0,8},{8,0},{1,9},{9,1},{2,10},{10,2},{3,11},{11,3},{4,12},{12,4},... | collective-permute-start | bytes 2949128 | tf_op jit(solution)/shard_map/ppermute | solution.py:51
  187.8 20.9 %all-to-all-start.5 = ((bf16[8,2,256,128]{3,2,1,0:T(8,128)(2,1)}), bf16[8,2,256,128]{3,2,1,0:T(8,128)(2,1)S(1)}, u32[]{:S(2)}, u32[]{:S(2)}) async-start(bf16[8,2,256,128]{3,2,1,0:T(8,128)(2,1)} %get-tuple-element.120), calls=%async_computation.5 | async-start | bytes 2097152 | tf_op jit(solution)/shard_map/all_to_all | solution.py:72
  208.7 25.8 %all-to-all-start.4 = ((bf16[8,3,256,128]{3,2,1,0:T(8,128)(2,1)}), bf16[8,3,256,128]{3,2,1,0:T(8,128)(2,1)S(1)}, u32[]{:S(2)}, u32[]{:S(2)}) async-start(bf16[8,3,256,128]{3,2,1,0:T(8,128)(2,1)} %get-tuple-element.117), calls=%async_computation.4 | async-start | bytes 3145728 | tf_op jit(solution)/shard_map/all_to_all | solution.py:72
  213.1 2.5 collective-permute-start.7
  214.1 33.2 %collective-permute-start.8 = (bf16[256,960]{1,0:T(8,128)(2,1)}, bf16[256,960]{1,0:T(8,128)(2,1)}, u32[]{:S(2)}, u32[]{:S(2)}) collective-permute-start(bf16[256,960]{1,0:T(8,128)(2,1)} %get-tuple-element.132.refs_0_), channel_id=1, source_target_pairs={{0,8},{8,0},{1,9},{9,1},{2,10},{10,2},{3,11},{11,3},{4,12},{12,4},... | collective-permute-start | bytes 1474568 | tf_op jit(solution)/shard_map/ppermute | solution.py:51
  234.5 31.0 %all-to-all-start.6 = ((bf16[16,64,640]{2,1,0:T(8,128)(2,1)}), bf16[16,64,640]{2,1,0:T(8,128)(2,1)S(1)}, u32[]{:S(2)}, u32[]{:S(2)}) async-start(bf16[16,64,640]{2,1,0:T(8,128)(2,1)} %pack_early.1), calls=%async_computation.8 | async-start | bytes 2621440 | tf_op jit(solution)/shard_map/all_to_all | solution.py:72
  246.5 13.6 %collective-permute-start.9 = (bf16[256,896]{1,0:T(8,128)(2,1)}, bf16[256,896]{1,0:T(8,128)(2,1)S(1)}, u32[]{:S(2)}, u32[]{:S(2)}) collective-permute-start(bf16[256,896]{1,0:T(8,128)(2,1)} %get-tuple-element.134), channel_id=1, source_target_pairs={{0,8},{8,0},{1,9},{9,1},{2,10},{10,2},{3,11},{11,3},{4,12},{12,4},... | collective-permute-start | bytes 1376264 | tf_op jit(solution)/shard_map/ppermute | solution.py:51
  265.5 74.9 %copy-start.8 = (f32[320,960]{1,0:T(8,128)S(1)}, f32[320,960]{1,0:T(8,128)}, u32[]{:S(2)}) copy-start(f32[320,960]{1,0:T(8,128)} %refs_11_.1) | copy-start | bytes 3686404
  265.5 74.8 %copy-start.9 = (f32[120,1600]{1,0:T(8,128)S(1)}, f32[120,1600]{1,0:T(8,128)}, u32[]{:S(2)}) copy-start(f32[120,1600]{1,0:T(8,128)} %refs_1_.3) | copy-start | bytes 2304004
  265.5 74.8 %copy-start.10 = (f32[120,1600]{1,0:T(8,128)S(1)}, f32[120,1600]{1,0:T(8,128)}, u32[]{:S(2)}) copy-start(f32[120,1600]{1,0:T(8,128)} %refs_2_.3) | copy-start | bytes 2304004
  265.5 74.8 %copy-start.13 = (f32[120,960]{1,0:T(8,128)S(1)}, f32[120,960]{1,0:T(8,128)}, u32[]{:S(2)}) copy-start(f32[120,960]{1,0:T(8,128)} %refs_5_.1) | copy-start | bytes 1382404
  305.4 35.0 %copy-start = (f32[120,5120]{1,0:T(8,128)S(1)}, f32[120,5120]{1,0:T(8,128)}, u32[]{:S(2)}) copy-start(f32[120,5120]{1,0:T(8,128)} %refs_6_.1) | copy-start | bytes 7372804
  305.4 35.0 %copy-start.3 = (f32[120,1600]{1,0:T(8,128)S(1)}, f32[120,1600]{1,0:T(8,128)}, u32[]{:S(2)}) copy-start(f32[120,1600]{1,0:T(8,128)} %refs_0_.1) | copy-start | bytes 2304004
  305.4 35.0 %copy-start.5 = (f32[120,5120]{1,0:T(8,128)S(1)}, f32[120,5120]{1,0:T(8,128)}, u32[]{:S(2)}) copy-start(f32[120,5120]{1,0:T(8,128)} %refs_8_.1) | copy-start | bytes 7372804
  305.4 35.0 %copy-start.7 = (f32[320,960]{1,0:T(8,128)S(1)}, f32[320,960]{1,0:T(8,128)}, u32[]{:S(2)}) copy-start(f32[320,960]{1,0:T(8,128)} %refs_10_.1) | copy-start | bytes 3686404
  305.4 35.0 %copy-start.12 = (f32[120,960]{1,0:T(8,128)S(1)}, f32[120,960]{1,0:T(8,128)}, u32[]{:S(2)}) copy-start(f32[120,960]{1,0:T(8,128)} %refs_4_.1) | copy-start | bytes 1382404
  305.9 34.5 %copy-start.4 = (f32[120,5120]{1,0:T(8,128)S(1)}, f32[120,5120]{1,0:T(8,128)}, u32[]{:S(2)}) copy-start(f32[120,5120]{1,0:T(8,128)} %refs_7_.1) | copy-start | bytes 7372804
  334.9 5.4 %collective-permute-start.12 = (bf16[4,128,1152]{2,1,0:T(8,128)(2,1)S(1)}, bf16[4,128,1152]{2,1,0:T(8,128)(2,1)S(1)}, u32[]{:S(2)}, u32[]{:S(2)}) collective-permute-start(bf16[4,128,1152]{2,1,0:T(8,128)(2,1)S(1)} %get-tuple-element.143.rest_ref), channel_id=1, source_target_pairs={{0,8},{8,0},{1,9},{9,1},{2,10},{10,2},{3,11},{11,3},{4,12},{12,4},... | collective-permute-start | bytes 3538952 | tf_op jit(solution)/shard_map/ppermute | solution.py:51
  337.5 2.8 collective-permute-start.11
  (26 other events, 111.9 us)
Sparse Core Ops, SparseCore 0:
  65.1 64.3 all-gather.2
  162.2 53.0 reduce-scatter.2
  217.9 42.2 reduce-scatter.4

commit v2 on v1

--- a/solution.py
+++ b/solution.py
@@ -917,25 +917,28 @@
     gains_ref[...] = jnp.concatenate(gains, axis=0)
 
 
-def weight_kernel(
-    normed_ref, normed_other, near_ref, came_ref, gains_ref, tall_ref, out_ref
-):
+def weight_kernel(normed_ref, normed_other, near_ref, came_ref, gains_ref, out_ref):
     columns = jnp.concatenate([normed_ref[...], normed_other[...]], axis=0).T
     product = contract(columns, jnp.concatenate([near_ref[...], came_ref[...]], axis=0), 1, 0)
-    groups = out_ref.shape[0] // 2
+    groups = out_ref.shape[0]
     shard = product.shape[0] // groups
     lanes = product.shape[1]
     gains = gains_ref[...]
-    quarter = FF // 64
-    down = tall_ref[: groups * quarter].astype(jnp.float32)
-    proj = tall_ref[groups * quarter :].astype(jnp.float32)
     for j in range(groups):
         span = slice(j * shard, (j + 1) * shard)
         tail = padded_rows(gains[:, span], 128 - shard)
         tail = jnp.concatenate(
             [tail, jnp.zeros((128 - shard, lanes - shard), jnp.float32)], axis=1
         )
-        summed = jnp.concatenate([product[span], tail], axis=0)
+        out_ref[j] = jnp.concatenate([product[span], tail], axis=0).astype(low)
+
+
+def pack_late_kernel(weight_ref, tall_ref, out_ref):
+    groups = weight_ref.shape[0]
+    quarter = FF // 64
+    down = tall_ref[: groups * quarter].astype(jnp.float32)
+    proj = tall_ref[groups * quarter :].astype(jnp.float32)
+    for j in range(groups):
         tall = jnp.concatenate(
             [down[j * quarter : (j + 1) * quarter], proj[j * 16 : (j + 1) * 16]], axis=0
         )
@@ -943,7 +946,8 @@
             jnp.concatenate([padded_rows(tall[:, span], 64) for span in spans], axis=0)
             for spans in (TALL_NARROW, TALL_WIDE)
         ]
-        put_halves(out_ref, j, jnp.concatenate([summed[:, : QKVW // 2]] + halves, axis=1))
+        weight = weight_ref[j].astype(jnp.float32)[:, : QKVW // 2]
+        put_halves(out_ref, j, jnp.concatenate([weight] + halves, axis=1))
 
 
 def padded_rows(block, rows):
@@ -1198,12 +1202,19 @@
         weight_kernel,
         "weight",
         1000,
-        jax.ShapeDtypeStruct((2 * groups, 64, LATE), low),
+        jax.ShapeDtypeStruct((groups, 128, PADDED), low),
         normed_one,
         normed_other,
         near,
         swap_cores(away),
         late_gains,
+    )
+    late = whole_call(
+        pack_late_kernel,
+        "pack_late",
+        1000,
+        jax.ShapeDtypeStruct((2 * groups, 64, LATE), low),
+        late,
         tall.reshape(groups * TALL, width),
     )
     late, early = lax.optimization_barrier((late, early))

time: 365 us -> 364 us (level)
  waiting for transfers between devices: 68.8 us -> 64.1 us
    reduce_scatter x1, waiting for transfers between devices: 12.9 us -> 6.54 us  [on_device(): tall = lax.psum_scatter(tall, 'y', scatter_dimension=0, tiled=False)]
    pallas_call x11 -> x12, Pallas kernels: 35.6 us -> 38.8 us  [whole_call(): pl.pallas_call(staged, out_shape=shapes, in_specs=[scalars() if value.ndi...]
  transfers between devices with their start and end apart: 22 -> 22, of which waited for: 12 -> 13; matrix products, arithmetic and copies ran while one was open for 1% -> 1% of each run, Pallas kernels for 23% -> 24%
where the time goes in v2:
time: 364 us; the launch traced here: 357 us
  Pallas kernels  120 us (33%)
  blocking collectives  105 us (29%)
  waiting for transfers between devices  64.1 us (18%)
  starting transfers between devices  39.1 us (11%)
  between operations  14.7 us (4%)
  local copies, waits for them, and re-layouts  11.5 us (3%)
    all_to_all x3, blocking collectives, exchange(): return lax.all_to_all(stack, axes, 0, 0, tiled=True)  105 us
    all_to_all x6, waiting for transfers between devices, exchange(): return lax.all_to_all(stack, axes, 0, 0, tiled=True)  43.5 us
    pallas_call x12, Pallas kernels, whole_call(): pl.pallas_call(staged, out_shape=shapes, in_specs=[scalars() if value.ndi...  38.8 us
    all_to_all x6, starting transfers between devices, exchange(): return lax.all_to_all(stack, axes, 0, 0, tiled=True)  28.6 us
    pallas_call x2, Pallas kernels, attend_back(): pl.pallas_call(attend_back_kernel, grid=(count,), out_shape=(jax.ShapeDty...  25.6 us
    pallas_call x1, Pallas kernels, feed(): pl.pallas_call(feed_kernel, grid=(2,), out_shape=(own, other, own, other,...  20 us
    pallas_call x1, Pallas kernels, attend(): pl.pallas_call(attend_kernel, grid=(KV_HEADS,), out_shape=(jax.ShapeDtype...  16.5 us
    ppermute x13, waiting for transfers between devices, swap_cores(): return lax.ppermute(value, 'core', [(0, 1), (1, 0)])  11.9 us
  transfers between devices with their start and end apart: 22, of which 13 were waited for; matrix products, arithmetic and copies ran while one was open for 1% of the time, Pallas kernels for 24%

profile of v2, /device:TPU:1, one launch (start us, length us, event | category | flops | bytes accessed | tf_op | source)
XLA Modules:
  0.0 356.7 jit_solution(3212554018121171835)
XLA Ops:
  7.2 2.6 stage.1
  9.8 6.2 %all-to-all-start = ((bf16[8,120,896]{2,1,0:T(8,128)(2,1)}), bf16[8,120,896]{2,1,0:T(8,128)(2,1)S(1)}, u32[]{:S(2)}, u32[]{:S(2)}) async-start(bf16[8,120,896]{2,1,0:T(8,128)(2,1)} %stage.1), calls=%async_computation | async-start | bytes 3440640 | tf_op jit(solution)/shard_map/all_to_all | solution.py:72
  16.6 4.9 %stage_feed.1 = (bf16[8,120,768]{2,1,0:T(8,128)(2,1)}, bf16[8,160,960]{2,1,0:T(8,128)(2,1)}) custom-call(s32[3]{0:T(128)} %pad_add_fusion.place_ref, f32[120,5120]{1,0:T(8,128)} %refs_6_.1, f32[320,960]{1,0:T(8,128)} %refs_9_.1, f32[120,960]{1,0:T(8,128)} %refs_3_.1), custom_call_target="tpu_custom_call" | custom-call | flops 1000 | bytes 8000000 | tf_op jit(solution)/shard_map/stage_feed/pallas_call | solution.py:405
  24.0 15.0 %all-to-all-done = bf16[8,120,896]{2,1,0:T(8,128)(2,1)S(1)} async-done(((bf16[8,120,896]{2,1,0:T(8,128)(2,1)}), bf16[8,120,896]{2,1,0:T(8,128)(2,1)S(1)}, u32[]{:S(2)}, u32[]{:S(2)}) %all-to-all-start) | async-done | bytes 1720352 | tf_op jit(solution)/shard_map/all_to_all | solution.py:72
  39.8 3.6 %all-to-all-start.1 = ((bf16[8,120,768]{2,1,0:T(8,128)(2,1)}), bf16[8,120,768]{2,1,0:T(8,128)(2,1)S(1)}, u32[]{:S(2)}, u32[]{:S(2)}) async-start(bf16[8,120,768]{2,1,0:T(8,128)(2,1)} %get-tuple-element.95), calls=%async_computation.1 | async-start | bytes 2949120 | tf_op jit(solution)/shard_map/all_to_all | solution.py:72
  43.5 5.8 %project.1 = (bf16[256,960]{1,0:T(8,128)(2,1)}, bf16[960,256]{1,0:T(8,128)(2,1)}, bf16[8,5,128,256]{3,2,1,0:T(8,128)(2,1)}, f32[2,960]{1,0:T(2,128)}) custom-call(s32[1]{0:T(128)} %bitcast.1.refs_0_.core_ref, bf16[960,256]{1,0:T(8,128)(2,1)} %bitcast.28, bf16[960,896]{1,0:T(8,128)(2,1)} %bitcast.25, bf16[960,896]{1,0:T(8,128)(2,1)} %collective-permute-done.refs_3_.refs_8_, ...), custom_call_target="tpu_custom_call" | custom-call | flops 1000 | bytes 1000 | tf_op jit(solution)/shard_map/project/pallas_call | solution.py:349
  49.3 14.6 %all-to-all-done.1 = bf16[8,120,768]{2,1,0:T(8,128)(2,1)S(1)} async-done(((bf16[8,120,768]{2,1,0:T(8,128)(2,1)}), bf16[8,120,768]{2,1,0:T(8,128)(2,1)S(1)}, u32[]{:S(2)}, u32[]{:S(2)}) %all-to-all-start.1) | async-done | bytes 1474592 | tf_op jit(solution)/shard_map/all_to_all | solution.py:72
  65.0 36.3 %all_to_all.45.kv_ref = bf16[8,5,128,256]{3,2,1,0:T(8,128)(2,1)} all-to-all(bf16[8,5,128,256]{3,2,1,0:T(8,128)(2,1)} %get-tuple-element.96), channel_id=1, replica_groups=mesh['zh'=2,'y'=4,'core'=2,'zl'=2,'x'=4] {'zl','x'}, dimensions={0} | all-to-all | bytes 5242880 | tf_op jit(solution)/shard_map/all_to_all | solution.py:72
  101.3 4.4 %all-to-all-start.3 = ((bf16[8,160,960]{2,1,0:T(8,128)(2,1)}), bf16[8,160,960]{2,1,0:T(8,128)(2,1)}, u32[]{:S(2)}, u32[]{:S(2)}) async-start(bf16[8,160,960]{2,1,0:T(8,128)(2,1)} %get-tuple-element.106), calls=%async_computation.3 | async-start | bytes 5242880 | tf_op jit(solution)/shard_map/all_to_all | solution.py:72
  105.8 16.5 %attend.1 = (bf16[960,256]{1,0:T(8,128)(2,1)}, f32[15,1,256]{2,1,0:T(1,128)}) custom-call(s32[16]{0:T(128)} %order_ref.5, s32[2]{0:T(128)} %get-tuple-element.160.own_ref, s32[1]{0:T(128)} %bitcast.rank_ref, bf16[960,256]{1,0:T(8,128)(2,1)} %get-tuple-element.93.q_ref, bf16[8,5,128,256]{3,2,1,0:T(8,128)(2,1)} %all_to_all.45.kv_ref), custom_call_target="tpu_custom_call" | custom-call | flops 20000000000 | bytes 1000 | tf_op jit(solution)/shard_map/attend/pallas_call | solution.py:275
  129.5 2.7 copy-done.1
  137.9 3.4 middle.1
  142.1 20.0 %feed.1 = (f32[256,960]{1,0:T(8,128)}, bf16[256,960]{1,0:T(8,128)(2,1)}, f32[256,960]{1,0:T(8,128)}, bf16[256,960]{1,0:T(8,128)(2,1)}, bf16[4,448,960]{2,1,0:T(8,128)(2,1)}, /*index=5*/bf16[4,960,640]{2,1,0:T(8,128)(2,1)}) custom-call(bf16[256,960]{1,0:T(8,128)(2,1)} %get-tuple-element.107.rows_one, bf16[256,960]{1,0:T(8,128)(2,1)} %get-tuple-element.108.rows_two, ...), custom_call_target="tpu_custom_call" | custom-call | flops 20000000000 | bytes 1000 | tf_op jit(solution)/shard_map/feed/pallas_call | solution.py:661
  166.3 6.2 %turn.1 = (f32[256,960]{1,0:T(8,128)}, bf16[960,256]{1,0:T(8,128)(2,1)}, bf16[8,64,960]{2,1,0:T(8,128)(2,1)}, bf16[8,64,960]{2,1,0:T(8,128)(2,1)}, f32[1,960]{1,0:T(1,128)}) custom-call(s32[1]{0:T(128)} %bitcast.1.refs_0_.core_ref, f32[256,960]{1,0:T(8,128)} %get-tuple-element.111.refs_1_, bf16[256,960]{1,0:T(8,128)(2,1)} %copy-done.35, ...), custom_call_target="tpu_custom_call" | custom-call | flops 3000000000 | bytes 1000 | tf_op jit(solution)/shard_map/turn/pallas_call | solution.py:349
  173.2 10.6 %attend_back_0.1 = (f32[384,256]{1,0:T(8,128)}, bf16[8,2,256,128]{3,2,1,0:T(8,128)(2,1)}) custom-call(s32[16]{0:T(128)} %order_ref.5, s32[2]{0:T(128)} %get-tuple-element.160.own_ref, s32[1]{0:T(128)} %bitcast.rank_ref, bf16[960,256]{1,0:T(8,128)(2,1)} %get-tuple-element.93.q_ref, bf16[8,5,128,256]{3,2,1,0:T(8,128)(2,1)} %all_to_all.45.kv_ref, ...), custom_call_target="tpu_custom_call" | custom-call | flops 10000000000 | bytes 1000 | tf_op jit(solution)/shard_map/attend_back_0/pallas_call | solution.py:298
  184.8 2.9 stack.17
  187.7 5.0 %all-to-all-start.5 = ((bf16[8,2,256,128]{3,2,1,0:T(8,128)(2,1)}), bf16[8,2,256,128]{3,2,1,0:T(8,128)(2,1)S(1)}, u32[]{:S(2)}, u32[]{:S(2)}) async-start(bf16[8,2,256,128]{3,2,1,0:T(8,128)(2,1)} %get-tuple-element.120), calls=%async_computation.5 | async-start | bytes 2097152 | tf_op jit(solution)/shard_map/all_to_all | solution.py:72
  192.8 15.0 %attend_back_2.1 = (f32[576,256]{1,0:T(8,128)}, bf16[8,3,256,128]{3,2,1,0:T(8,128)(2,1)}) custom-call(s32[16]{0:T(128)} %order_ref.5, s32[2]{0:T(128)} %get-tuple-element.160.own_ref, s32[1]{0:T(128)} %bitcast.rank_ref, bf16[960,256]{1,0:T(8,128)(2,1)} %get-tuple-element.93.q_ref, bf16[8,5,128,256]{3,2,1,0:T(8,128)(2,1)} %all_to_all.45.kv_ref, ...), custom_call_target="tpu_custom_call" | custom-call | flops 15000000512 | bytes 1000 | tf_op jit(solution)/shard_map/attend_back_2/pallas_call | solution.py:298
  208.6 4.4 %all-to-all-start.4 = ((bf16[8,3,256,128]{3,2,1,0:T(8,128)(2,1)}), bf16[8,3,256,128]{3,2,1,0:T(8,128)(2,1)S(1)}, u32[]{:S(2)}, u32[]{:S(2)}) async-start(bf16[8,3,256,128]{3,2,1,0:T(8,128)(2,1)} %get-tuple-element.117), calls=%async_computation.4 | async-start | bytes 3145728 | tf_op jit(solution)/shard_map/all_to_all | solution.py:72
  216.4 2.7 emit.1
  219.1 2.5 pack_early.1
  221.6 12.9 %all-to-all-done.4.refs_2_ = bf16[8,3,256,128]{3,2,1,0:T(8,128)(2,1)S(1)} async-done(((bf16[8,3,256,128]{3,2,1,0:T(8,128)(2,1)}), bf16[8,3,256,128]{3,2,1,0:T(8,128)(2,1)S(1)}, u32[]{:S(2)}, u32[]{:S(2)}) %all-to-all-start.4) | async-done | bytes 1572896 | tf_op jit(solution)/shard_map/all_to_all | solution.py:72
  234.5 5.0 %all-to-all-start.6 = ((bf16[16,64,640]{2,1,0:T(8,128)(2,1)}), bf16[16,64,640]{2,1,0:T(8,128)(2,1)S(1)}, u32[]{:S(2)}, u32[]{:S(2)}) async-start(bf16[16,64,640]{2,1,0:T(8,128)(2,1)} %pack_early.1), calls=%async_computation.8 | async-start | bytes 2621440 | tf_op jit(solution)/shard_map/all_to_all | solution.py:72
  239.4 7.0 %late.1 = (bf16[960,256]{1,0:T(8,128)(2,1)}, bf16[256,896]{1,0:T(8,128)(2,1)}, bf16[256,896]{1,0:T(8,128)(2,1)}, f32[2,960]{1,0:T(2,128)}) custom-call(s32[1]{0:T(128)} %bitcast.1.refs_0_.core_ref, bf16[8,2,256,128]{3,2,1,0:T(8,128)(2,1)} %copy-done.24, bf16[8,3,256,128]{3,2,1,0:T(8,128)(2,1)} %copy-done.22, f32[384,256]{1,0:T(8,128)} %get-tuple-element.127.refs_3_, ...), custom_call_target="tpu_custom_call" | custom-call | flops 30000001024 | bytes 1000 | tf_op jit(solution)/shard_map/late/pallas_call | solution.py:349
  249.6 4.0 %weight.1.refs_0_ = bf16[8,128,896]{2,1,0:T(8,128)(2,1)} custom-call(bf16[256,960]{1,0:T(8,128)(2,1)} %get-tuple-element.132.refs_0_, bf16[256,960]{1,0:T(8,128)(2,1)} %collective-permute-done.8.refs_1_, bf16[256,896]{1,0:T(8,128)(2,1)} %get-tuple-element.133.refs_2_, bf16[256,896]{1,0:T(8,128)(2,1)} %copy-done.29, f32[2,960]{1,0:T(2,128)} %get-tuple-element.135.refs_4_), custom_call_target="tpu_custom_call" | custom-call | flops 1000 | bytes 1000 | tf_op jit(solution)/shard_map/weight/pallas_call | solution.py:349
  253.6 6.5 %reduce-scatter.5.cloned.1.call-done = bf16[1,448,960]{2,1,0:T(8,128)(2,1)} async-done(((bf16[4,448,960]{2,1,0:T(8,128)(2,1)}), bf16[1,448,960]{2,1,0:T(8,128)(2,1)}) %reduce-scatter.5.cloned.1.call-update) | async-done | bytes 860176 | tf_op jit(solution)/shard_map/reduce_scatter | solution.py:1175
  260.1 3.8 %pack_late.1 = bf16[16,64,1280]{2,1,0:T(8,128)(2,1)} custom-call(bf16[8,128,896]{2,1,0:T(8,128)(2,1)} %weight.1.refs_0_, bf16[448,960]{1,0:T(8,128)(2,1)} %bitcast.33), custom_call_target="tpu_custom_call" | custom-call | flops 1000 | bytes 1000 | tf_op jit(solution)/shard_map/pack_late/pallas_call | solution.py:349
  264.0 39.8 %all_to_all.46.refs_1_ = bf16[16,64,1280]{2,1,0:T(8,128)(2,1)S(1)} all-to-all(bf16[16,64,1280]{2,1,0:T(8,128)(2,1)} %pack_late.1), channel_id=1, replica_groups=mesh['zh'=2,'y'=4,'core'=2,'zl'=2,'x'=4] {'zh','zl','x'}, dimensions={0} | all-to-all | bytes 5242880 | tf_op jit(solution)/shard_map/all_to_all | solution.py:72
  304.4 28.8 %all_to_all.47.refs_0_ = bf16[8,64,1920]{2,1,0:T(8,128)(2,1)S(1)} all-to-all(bf16[8,64,1920]{2,1,0:T(8,128)(2,1)S(1)} %sum_parts.1), channel_id=1, replica_groups=mesh['zh'=2,'y'=4,'core'=2,'zl'=2,'x'=4] {'zh','y'}, dimensions={0} | all-to-all | bytes 3932160 | tf_op jit(solution)/shard_map/all_to_all | solution.py:72
  333.3 2.6 collective-permute-start.12
  336.1 2.7 collective-permute-done.11.wide_other
  338.9 10.8 %update.1 = (f32[120,1600]{1,0:T(8,128)}, f32[120,1600]{1,0:T(8,128)}, f32[120,1600]{1,0:T(8,128)}, f32[120,960]{1,0:T(8,128)}, f32[120,960]{1,0:T(8,128)}, /*in...) custom-call(s32[1]{0:T(128)} %bitcast.1.refs_0_.core_ref, ...), custom_call_target="tpu_custom_call" | custom-call | flops 1000 | bytes 30000000 | tf_op jit(solution)/shard_map/update/pallas_call | solution.py:840
  (116 shorter events, 33.0 us)
Async XLA Ops:
  9.8 29.2 %all-to-all-start = ((bf16[8,120,896]{2,1,0:T(8,128)(2,1)}), bf16[8,120,896]{2,1,0:T(8,128)(2,1)S(1)}, u32[]{:S(2)}, u32[]{:S(2)}) async-start(bf16[8,120,896]{2,1,0:T(8,128)(2,1)} %stage.1), calls=%async_computation | async-start | bytes 3440640 | tf_op jit(solution)/shard_map/all_to_all | solution.py:72
  39.0 4.5 %collective-permute-start = (bf16[960,896]{1,0:T(8,128)(2,1)S(1)}, bf16[960,896]{1,0:T(8,128)(2,1)}, u32[]{:S(2)}, u32[]{:S(2)}) collective-permute-start(bf16[960,896]{1,0:T(8,128)(2,1)S(1)} %bitcast.24), channel_id=1, source_target_pairs={{0,8},{8,0},{1,9},{9,1},{2,10},{10,2},{3,11},{11,3},{4,12},{12,4},... | collective-permute-start | bytes 5160968 | tf_op jit(solution)/shard_map/ppermute | solution.py:51
  39.8 24.0 %all-to-all-start.1 = ((bf16[8,120,768]{2,1,0:T(8,128)(2,1)}), bf16[8,120,768]{2,1,0:T(8,128)(2,1)S(1)}, u32[]{:S(2)}, u32[]{:S(2)}) async-start(bf16[8,120,768]{2,1,0:T(8,128)(2,1)} %get-tuple-element.95), calls=%async_computation.1 | async-start | bytes 2949120 | tf_op jit(solution)/shard_map/all_to_all | solution.py:72
  43.4 86.1 %all-gather.3.cloned.1.call-start = ((), (), s32[]{:S(2)}) async-start(), calls=%async_computation.13 | async-start | bytes 7372800 | tf_op jit(solution)/shard_map/all_gather | solution.py:1082
  101.3 39.9 %all-to-all-start.3 = ((bf16[8,160,960]{2,1,0:T(8,128)(2,1)}), bf16[8,160,960]{2,1,0:T(8,128)(2,1)}, u32[]{:S(2)}, u32[]{:S(2)}) async-start(bf16[8,160,960]{2,1,0:T(8,128)(2,1)} %get-tuple-element.106), calls=%async_computation.3 | async-start | bytes 5242880 | tf_op jit(solution)/shard_map/all_to_all | solution.py:72
  105.7 113.4 %reduce-scatter.3.cloned.1.call-start = ((), (), s32[]{:S(2)}) async-start(), calls=%async_computation.11 | async-start | bytes 6144000 | tf_op jit(solution)/shard_map/reduce_scatter | solution.py:1156
  122.2 3.7 %collective-permute-start.1 = (bf16[960,256]{1,0:T(8,128)(2,1)}, bf16[960,256]{1,0:T(8,128)(2,1)S(1)}, u32[]{:S(2)}, u32[]{:S(2)}) collective-permute-start(bf16[960,256]{1,0:T(8,128)(2,1)} %get-tuple-element.99.refs_0_.refs_8_.o_ref), channel_id=1, source_target_pairs={{0,8},{8,0},{1,9},{9,1},{2,10},{10,2},{3,11},{11,3},{4,12},{12,4},... | collective-permute-start | bytes 1474568 | tf_op jit(solution)/shard_map/ppermute | solution.py:51
  133.2 3.7 %collective-permute-start.2 = (bf16[512,512]{1,0:T(8,128)(2,1)S(1)}, bf16[512,512]{1,0:T(8,128)(2,1)S(1)}, u32[]{:S(2)}, u32[]{:S(2)}) collective-permute-start(bf16[512,512]{1,0:T(8,128)(2,1)S(1)} %get-tuple-element.103.refs_1_), channel_id=1, source_target_pairs={{0,8},{8,0},{1,9},{9,1},{2,10},{10,2},{3,11},{11,3},{4,12},{12,4},... | collective-permute-start | bytes 1572872 | tf_op jit(solution)/shard_map/ppermute | solution.py:51
  134.0 2.9 collective-permute-start.3
  134.1 7.2 %collective-permute-start.4 = (bf16[256,960]{1,0:T(8,128)(2,1)}, bf16[256,960]{1,0:T(8,128)(2,1)S(1)}, u32[]{:S(2)}, u32[]{:S(2)}) collective-permute-start(bf16[256,960]{1,0:T(8,128)(2,1)} %bitcast.8.back_one.refs_4_), channel_id=1, source_target_pairs={{0,8},{8,0},{1,9},{9,1},{2,10},{10,2},{3,11},{11,3},{4,12},{12,4},... | collective-permute-start | bytes 1474568 | tf_op jit(solution)/shard_map/ppermute | solution.py:51
  162.1 98.0 %reduce-scatter.5.cloned.1.call-start = ((), (), s32[]{:S(2)}) async-start(), calls=%async_computation.12 | async-start | bytes 4587520 | tf_op jit(solution)/shard_map/reduce_scatter | solution.py:1175
  162.2 2.7 collective-permute-start.6
  163.1 2.4 collective-permute-start.5
  172.5 11.3 %collective-permute-start.10 = (bf16[8,64,960]{2,1,0:T(8,128)(2,1)}, bf16[8,64,960]{2,1,0:T(8,128)(2,1)S(1)}, u32[]{:S(2)}, u32[]{:S(2)}) collective-permute-start(bf16[8,64,960]{2,1,0:T(8,128)(2,1)} %get-tuple-element.138), channel_id=1, source_target_pairs={{0,8},{8,0},{1,9},{9,1},{2,10},{10,2},{3,11},{11,3},{4,12},{12,4},... | collective-permute-start | bytes 2949128 | tf_op jit(solution)/shard_map/ppermute | solution.py:51
  187.7 20.9 %all-to-all-start.5 = ((bf16[8,2,256,128]{3,2,1,0:T(8,128)(2,1)}), bf16[8,2,256,128]{3,2,1,0:T(8,128)(2,1)S(1)}, u32[]{:S(2)}, u32[]{:S(2)}) async-start(bf16[8,2,256,128]{3,2,1,0:T(8,128)(2,1)} %get-tuple-element.120), calls=%async_computation.5 | async-start | bytes 2097152 | tf_op jit(solution)/shard_map/all_to_all | solution.py:72
  208.6 25.8 %all-to-all-start.4 = ((bf16[8,3,256,128]{3,2,1,0:T(8,128)(2,1)}), bf16[8,3,256,128]{3,2,1,0:T(8,128)(2,1)S(1)}, u32[]{:S(2)}, u32[]{:S(2)}) async-start(bf16[8,3,256,128]{3,2,1,0:T(8,128)(2,1)} %get-tuple-element.117), calls=%async_computation.4 | async-start | bytes 3145728 | tf_op jit(solution)/shard_map/all_to_all | solution.py:72
  213.0 2.5 collective-permute-start.7
  214.0 33.2 %collective-permute-start.8 = (bf16[256,960]{1,0:T(8,128)(2,1)}, bf16[256,960]{1,0:T(8,128)(2,1)}, u32[]{:S(2)}, u32[]{:S(2)}) collective-permute-start(bf16[256,960]{1,0:T(8,128)(2,1)} %get-tuple-element.132.refs_0_), channel_id=1, source_target_pairs={{0,8},{8,0},{1,9},{9,1},{2,10},{10,2},{3,11},{11,3},{4,12},{12,4},... | collective-permute-start | bytes 1474568 | tf_op jit(solution)/shard_map/ppermute | solution.py:51
  234.5 29.5 %all-to-all-start.6 = ((bf16[16,64,640]{2,1,0:T(8,128)(2,1)}), bf16[16,64,640]{2,1,0:T(8,128)(2,1)S(1)}, u32[]{:S(2)}, u32[]{:S(2)}) async-start(bf16[16,64,640]{2,1,0:T(8,128)(2,1)} %pack_early.1), calls=%async_computation.8 | async-start | bytes 2621440 | tf_op jit(solution)/shard_map/all_to_all | solution.py:72
  246.5 2.4 collective-permute-start.9
  264.0 74.8 %copy-start.8 = (f32[320,960]{1,0:T(8,128)S(1)}, f32[320,960]{1,0:T(8,128)}, u32[]{:S(2)}) copy-start(f32[320,960]{1,0:T(8,128)} %refs_11_.1) | copy-start | bytes 3686404
  264.0 74.8 %copy-start.9 = (f32[120,1600]{1,0:T(8,128)S(1)}, f32[120,1600]{1,0:T(8,128)}, u32[]{:S(2)}) copy-start(f32[120,1600]{1,0:T(8,128)} %refs_1_.3) | copy-start | bytes 2304004
  264.0 74.8 %copy-start.10 = (f32[120,1600]{1,0:T(8,128)S(1)}, f32[120,1600]{1,0:T(8,128)}, u32[]{:S(2)}) copy-start(f32[120,1600]{1,0:T(8,128)} %refs_2_.3) | copy-start | bytes 2304004
  264.0 74.8 %copy-start.13 = (f32[120,960]{1,0:T(8,128)S(1)}, f32[120,960]{1,0:T(8,128)}, u32[]{:S(2)}) copy-start(f32[120,960]{1,0:T(8,128)} %refs_5_.1) | copy-start | bytes 1382404
  303.8 35.0 %copy-start = (f32[120,5120]{1,0:T(8,128)S(1)}, f32[120,5120]{1,0:T(8,128)}, u32[]{:S(2)}) copy-start(f32[120,5120]{1,0:T(8,128)} %refs_6_.1) | copy-start | bytes 7372804
  303.8 35.0 %copy-start.3 = (f32[120,1600]{1,0:T(8,128)S(1)}, f32[120,1600]{1,0:T(8,128)}, u32[]{:S(2)}) copy-start(f32[120,1600]{1,0:T(8,128)} %refs_0_.1) | copy-start | bytes 2304004
  303.8 35.0 %copy-start.5 = (f32[120,5120]{1,0:T(8,128)S(1)}, f32[120,5120]{1,0:T(8,128)}, u32[]{:S(2)}) copy-start(f32[120,5120]{1,0:T(8,128)} %refs_8_.1) | copy-start | bytes 7372804
  303.8 35.0 %copy-start.7 = (f32[320,960]{1,0:T(8,128)S(1)}, f32[320,960]{1,0:T(8,128)}, u32[]{:S(2)}) copy-start(f32[320,960]{1,0:T(8,128)} %refs_10_.1) | copy-start | bytes 3686404
  303.8 35.0 %copy-start.12 = (f32[120,960]{1,0:T(8,128)S(1)}, f32[120,960]{1,0:T(8,128)}, u32[]{:S(2)}) copy-start(f32[120,960]{1,0:T(8,128)} %refs_4_.1) | copy-start | bytes 1382404
  304.4 34.5 %copy-start.4 = (f32[120,5120]{1,0:T(8,128)S(1)}, f32[120,5120]{1,0:T(8,128)}, u32[]{:S(2)}) copy-start(f32[120,5120]{1,0:T(8,128)} %refs_7_.1) | copy-start | bytes 7372804
  333.3 5.4 %collective-permute-start.12 = (bf16[4,128,1152]{2,1,0:T(8,128)(2,1)S(1)}, bf16[4,128,1152]{2,1,0:T(8,128)(2,1)S(1)}, u32[]{:S(2)}, u32[]{:S(2)}) collective-permute-start(bf16[4,128,1152]{2,1,0:T(8,128)(2,1)S(1)} %get-tuple-element.143.rest_ref), channel_id=1, source_target_pairs={{0,8},{8,0},{1,9},{9,1},{2,10},{10,2},{3,11},{11,3},{4,12},{12,4},... | collective-permute-start | bytes 3538952 | tf_op jit(solution)/shard_map/ppermute | solution.py:51
  336.0 2.8 collective-permute-start.11
  (26 other events, 111.8 us)
Sparse Core Ops, SparseCore 0:
  65.1 64.3 all-gather.2
  162.2 53.0 reduce-scatter.2
  217.8 42.2 reduce-scatter.4
